TPU v7x, 128 devices: a whole 4x4x4 slice. The times are simulated.
128 devices in a mesh: row: 16 (over x_lo, z, core), col: 8 (over x_hi, y).
Axes of the slice: x: 4 (x_hi: 2, x_lo: 2; x = x_hi * 2 + x_lo), y: 4, z: 4, core: 2. Of those that a mesh axis runs over, the one named last changes fastest.
Arguments:
- atom_single: bfloat16 [16384, 128], P(('row', 'col')), may hold values from -60 to 60
- atom_to_token: int32 [16384], replicated, may hold values from 0 to 2047, as said below
- token_mask: int32 [2048], P('col'), may hold values 0 or 1
- pair: bfloat16 [2048, 2048, 128], P('row', 'col'), may hold values from -16 to 16
- w_atom_qkv: bfloat16 [128, 384], replicated, may hold values from -0.5 to 0.5
- w_atom_out: bfloat16 [128, 128], replicated, may hold values from -0.5 to 0.5
- w_aggregate: bfloat16 [128, 768], replicated, may hold values from -0.5 to 0.5
- pair_gain: float32 [128], replicated, may hold values from 0.1 to 1.9
- w_pair_in: bfloat16 [128, 512], replicated, may hold values from -0.5 to 0.5
- w_pair_out: bfloat16 [256, 128], replicated, may hold values from -0.375 to 0.375
- bias_gain: float32 [128], replicated, may hold values from 0.15 to 200
- w_bias: bfloat16 [128, 16], replicated, may hold values from -2 to 2
- token_gain: float32 [768], replicated, may hold values from 0.1 to 1.9
- w_token_qkv: bfloat16 [768, 2304], replicated, may hold values from -0.21875 to 0.21875
- w_token_out: bfloat16 [768, 768], replicated, may hold values from -0.21875 to 0.21875
Outputs:
- atom_out: bfloat16 [16384, 128], P(('row', 'col'))
- token_out: bfloat16 [2048, 768], P(('row', 'col'))
- pair_out: bfloat16 [2048, 2048, 128], P('row', 'col')
Inputs may be any that keep to these rules, and one draw needn't show every extreme that they name: `atom_to_token`: never falling; every token 0 to 2047 has 1 to 24 atoms, some token exactly 24.
All inputs are finite; a program needn't handle non-finite values. No bound on the sum of `token_mask` on one device may be relied on, other than what follows from the above.
Results may differ from a plain program's by a relative error of at most 0.018.
Values may be sent and summed in bfloat16 or wider, within the bound.
A program may use at most 128 MiB of HBM per device.

v0:
```python
import jax
import jax.numpy as jnp
from jax import lax
from jax.sharding import PartitionSpec as P

ATOM_QUERIES = 32
ATOM_KEYS = 128


def with_halo(block, sides, width):
    for axis, dim in sides:
        count = lax.axis_size(axis)
        forward = [(i, i + 1) for i in range(count - 1)]
        backward = [(target, source) for source, target in forward]
        low = lax.ppermute(
            lax.slice_in_dim(block, block.shape[dim] - width, None, axis=dim), axis, forward
        )
        high = lax.ppermute(lax.slice_in_dim(block, 0, width, axis=dim), axis, backward)
        block = jnp.concatenate([low, block, high], axis=dim)
    return block


def layer_norm(x, gain):
    mean = jnp.mean(x, axis=-1, keepdims=True)
    var = jnp.mean((x - mean) ** 2, axis=-1, keepdims=True)
    return (x - mean) / jnp.sqrt(var + 1e-05) * gain


def body(
    atom_single,
    atom_to_token,
    token_mask,
    pair,
    w_atom_qkv,
    w_atom_out,
    w_aggregate,
    pair_gain,
    w_pair_in,
    w_pair_out,
    bias_gain,
    w_bias,
    token_gain,
    w_token_qkv,
    w_token_out,
):
    n_atoms = atom_single.shape[0]
    width_a = atom_single.shape[1]
    devices = lax.axis_size(("row", "col"))
    me_flat = lax.axis_index(("row", "col"))
    me_col = lax.axis_index("col")
    key_block = token_mask.shape[0]
    tok_here = key_block // lax.axis_size("row")
    width_t = w_token_out.shape[0]
    heads_t = w_bias.shape[1]
    head_t = width_t // heads_t
    heads_a = 4
    head_a = width_a // heads_a
    hidden_pair = w_pair_out.shape[0]
    atom_qkv = jnp.dot(atom_single, w_atom_qkv, preferred_element_type=jnp.float32).astype(
        jnp.bfloat16
    )
    padded = with_halo(atom_qkv[:, width_a:], ((("row", "col"), 0),), 48)
    nblock = n_atoms // ATOM_QUERIES
    index = (
        ATOM_QUERIES * jnp.arange(nblock, dtype=jnp.int32)[:, None]
        + jnp.arange(ATOM_KEYS, dtype=jnp.int32)[None, :]
    )
    window = padded[index]
    query = atom_qkv[:, :width_a].reshape(nblock, ATOM_QUERIES, heads_a, head_a)
    keys = window[:, :, :width_a].reshape(nblock, ATOM_KEYS, heads_a, head_a)
    values = window[:, :, width_a:].reshape(nblock, ATOM_KEYS, heads_a, head_a)
    place = index - 48 + me_flat * n_atoms
    outside = jnp.where((place >= 0) & (place < n_atoms * devices), 0.0, -1000000000.0).astype(
        jnp.float32
    )
    scores = jnp.einsum(
        "bqhd,bkhd->bhqk", query, keys, preferred_element_type=jnp.float32
    ) / jnp.sqrt(jnp.float32(head_a))
    scores = scores + outside[:, None, None, :]
    expo = jnp.exp(scores - jnp.max(scores, axis=-1, keepdims=True))
    total = jnp.sum(expo, axis=-1)
    numer = jnp.einsum(
        "bhqk,bkhd->bqhd", expo.astype(jnp.bfloat16), values, preferred_element_type=jnp.float32
    )
    atom_mix = (
        (numer / jnp.transpose(total, (0, 2, 1))[..., None])
        .astype(jnp.bfloat16)
        .reshape(n_atoms, width_a)
    )
    atom_out = (
        atom_single.astype(jnp.float32)
        + jnp.dot(atom_mix, w_atom_out, preferred_element_type=jnp.float32)
    ).astype(jnp.bfloat16)
    my_tokens = me_flat * tok_here + jnp.arange(tok_here, dtype=jnp.int32)
    counts = jnp.sum((atom_to_token[None, :] == my_tokens[:, None]).astype(jnp.float32), axis=1)
    atom_proj = jax.nn.relu(
        jnp.dot(atom_out, w_aggregate, preferred_element_type=jnp.float32)
    ).astype(jnp.bfloat16)
    local_ids = lax.dynamic_slice_in_dim(atom_to_token, me_flat * n_atoms, n_atoms, 0)
    wanted = jnp.arange(tok_here * lax.axis_size(("row", "col")), dtype=jnp.int32)
    onehot = (local_ids[None, :] == wanted[:, None]).astype(jnp.bfloat16)
    sums = lax.psum_scatter(
        jnp.dot(onehot, atom_proj, preferred_element_type=jnp.float32),
        ("row", "col"),
        scatter_dimension=0,
        tiled=True,
    )
    token_in = (sums / counts[:, None]).astype(jnp.bfloat16)

    def pair_rows(block):
        normed = layer_norm(block.astype(jnp.float32), pair_gain).astype(jnp.bfloat16)
        both = jnp.dot(normed, w_pair_in, preferred_element_type=jnp.float32)
        hidden = (jax.nn.silu(both[..., :hidden_pair]) * both[..., hidden_pair:]).astype(
            jnp.bfloat16
        )
        new_pair = (
            block.astype(jnp.float32)
            + jnp.dot(hidden, w_pair_out, preferred_element_type=jnp.float32)
        ).astype(jnp.bfloat16)
        normed_two = layer_norm(new_pair.astype(jnp.float32), bias_gain).astype(jnp.bfloat16)
        bias = jnp.dot(normed_two, w_bias, preferred_element_type=jnp.float32)
        return (new_pair, bias)

    query_block = pair.shape[0]
    pair_chan = pair.shape[2]
    pair_out, pair_bias = lax.map(
        pair_rows, pair.reshape(query_block // 16, 16, key_block, pair_chan)
    )
    pair_out = pair_out.reshape(query_block, key_block, pair_chan)
    pair_bias = pair_bias.reshape(query_block, key_block, heads_t)
    token_norm = layer_norm(token_in.astype(jnp.float32), token_gain).astype(jnp.bfloat16)
    token_qkv = jnp.dot(token_norm, w_token_qkv, preferred_element_type=jnp.float32).astype(
        jnp.bfloat16
    )
    queries = lax.all_gather(token_qkv[:, :width_t], "col", axis=0, tiled=True)
    everyone = lax.all_gather(token_qkv[:, width_t:], ("row", "col"), axis=0, tiled=True)
    mine = lax.dynamic_slice_in_dim(everyone, me_col * key_block, key_block, 0)
    tkeys = mine[:, :width_t].reshape(key_block, heads_t, head_t)
    tvalues = mine[:, width_t:].reshape(key_block, heads_t, head_t)
    masking = (token_mask.astype(jnp.float32) - 1.0) * 1000000000.0
    tscores = jnp.einsum(
        "qhd,khd->hqk",
        queries.reshape(query_block, heads_t, head_t),
        tkeys,
        preferred_element_type=jnp.float32,
    ) / jnp.sqrt(jnp.float32(head_t))
    tscores = tscores + jnp.transpose(pair_bias, (2, 0, 1)) + masking[None, None, :]
    largest = lax.pmax(jnp.max(tscores, axis=-1), "col")
    texpo = jnp.exp(tscores - largest[..., None])
    local_total = jnp.sum(texpo, axis=-1)
    local_numer = jnp.einsum(
        "hqk,khd->qhd", texpo.astype(jnp.bfloat16), tvalues, preferred_element_type=jnp.float32
    )
    tnumer, ttotal = (
        lax.psum(local_numer.astype(jnp.bfloat16), "col").astype(jnp.float32),
        lax.psum(local_total.astype(jnp.bfloat16), "col").astype(jnp.float32),
    )
    token_mix = (
        (tnumer / jnp.transpose(ttotal)[..., None])
        .astype(jnp.bfloat16)
        .reshape(query_block, width_t)
    )
    my_mix = lax.dynamic_slice_in_dim(token_mix, me_col * tok_here, tok_here, 0)
    token_out = (
        token_in.astype(jnp.float32)
        + jnp.dot(my_mix, w_token_out, preferred_element_type=jnp.float32)
    ).astype(jnp.bfloat16)
    return (atom_out, token_out, pair_out)


def solution(mesh):
    placed = (
        P(("row", "col"), None),
        P(),
        P("col"),
        P("row", "col", None),
        P(),
        P(),
        P(),
        P(),
        P(),
        P(),
        P(),
        P(),
        P(),
        P(),
        P(),
    )
    return jax.shard_map(
        body,
        mesh=mesh,
        in_specs=placed,
        out_specs=(P(("row", "col"), None), P(("row", "col"), None), P("row", "col", None)),
        check_vma=False,
    )
```

profile of v0, /device:TPU:0, one launch (start us, length us, event | category | flops | bytes accessed | tf_op | source)
XLA Modules:
  0.0 1132.9 jit_solution(17533155900624636935)
XLA Ops:
  11.0 5.2 collective-permute-start
  22.9 3.1 gather_fusion
  39.3 4.8 fusion.37
  44.2 11.9 %copy.52 = bf16[128,256,128]{1,2,0:T(8,128)(2,1)} copy(bf16[128,256,128]{2,1,0:T(8,128)(2,1)} %param.20) | data formatting | bytes 16777216 | tf_op args[3]
  58.9 638.2 %reduce-scatter.2.cloned.1.call-done = f32[16,768]{1,0:T(8,128)} async-done(((f32[2048,768]{1,0:T(8,128)}), f32[16,768]{1,0:T(8,128)}) %reduce-scatter.2.cloned.1.call-update) | async-done | bytes 49168 | tf_op jit(solution)/shard_map/reduce_scatter | solution.py:102
  700.7 126.8 %while.12 = (s32[]{:T(128)}, bf16[8,16,256,128]{3,2,1,0:T(8,128)(2,1)}, f32[8,16,256,16]{2,1,0,3:T(8,128)}, bf16[8,16,256,128]{2,3,1,0:T(8,128)(2,1)}, f32[128]{...) while((s32[]{:T(128)}, ...), condition=%wide.region_11.12_spmd, body=%wide.region_6.11_spmd.sunk | while | flops 841490432 | bytes 34596148 | solution.py:126
  703.7 2.6 fusion.96
  706.4 3.8 convert_reduce_fusion.7
  719.6 2.6 fusion.96
  722.2 3.8 convert_reduce_fusion.7
  735.5 2.6 fusion.96
  738.1 3.8 convert_reduce_fusion.7
  753.9 3.8 convert_reduce_fusion.7
  769.8 3.8 convert_reduce_fusion.7
  785.6 3.8 convert_reduce_fusion.7
  801.5 3.8 convert_reduce_fusion.7
  817.3 3.8 convert_reduce_fusion.7
  828.9 36.4 %all_gather.7 = bf16[128,768]{1,0:T(8,128)(2,1)} all-gather(bf16[16,768]{1,0:T(8,128)(2,1)S(1)} %slice.59), channel_id=1, replica_groups=mesh['row'=16,'col'=8] {'col'}, dimensions={0}, use_global_device_ids=true | all-gather | bytes 221184 | tf_op jit(solution)/shard_map/all_gather | solution.py:135
  867.0 138.2 %all-gather.2.cloned.1.call-done = bf16[2048,1536]{1,0:T(8,128)(2,1)} async-done(((bf16[16,1536]{1,0:T(8,128)(2,1)}), bf16[2048,1536]{1,0:T(8,128)(2,1)}) %all-gather.2.cloned.1.call-update) | async-done | bytes 6291472 | tf_op jit(solution)/shard_map/all_gather | solution.py:136
  1011.1 3.7 fusion.70
  1014.8 23.5 %pmax.7 = f32[16,128]{1,0:T(8,128)S(1)} all-reduce(f32[16,128]{1,0:T(8,128)S(1)} %get-tuple-element.110), channel_id=1, replica_groups=mesh['row'=16,'col'=8] {'col'}, use_global_device_ids=true, to_apply=%region_13.14 | all-reduce | flops 2048 | bytes 16384 | tf_op jit(solution)/shard_map/pmax | solution.py:148
  1038.3 3.0 fusion.38
  1043.6 19.0 %psum.15 = bf16[128,16]{0,1:T(8,128)(2,1)S(1)} all-reduce(bf16[128,16]{0,1:T(8,128)(2,1)S(1)} %bitcast.98), channel_id=1, replica_groups=mesh['row'=16,'col'=8] {'col'}, use_global_device_ids=true, to_apply=%region_16.17 | all-reduce | flops 2048 | bytes 8192 | tf_op jit(solution)/shard_map/psum | solution.py:156
  1062.6 60.5 %all-reduce.2.cloned.1.call-done = bf16[128,16,48]{0,2,1:T(8,128)(2,1)} async-done(((bf16[128,16,48]{0,2,1:T(8,128)(2,1)}), bf16[128,16,48]{0,2,1:T(8,128)(2,1)}) %all-reduce.2.cloned.1.call-update) | async-done | bytes 196624 | tf_op jit(solution)/shard_map/psum | solution.py:155
  (251 shorter events, 132.4 us)
Async XLA Ops:
  7.2 691.5 %copy-start = (bf16[768,2304]{1,0:T(8,128)(2,1)S(1)}, bf16[768,2304]{1,0:T(8,128)(2,1)}, u32[]{:S(2)}) copy-start(bf16[768,2304]{1,0:T(8,128)(2,1)} %param.30) | copy-start | bytes 10616836
  7.2 689.9 %reduce-scatter.2.cloned.1.call-start = ((), (), s32[]{:S(2)}) async-start(), calls=%async_computation.1 | async-start | bytes 6340608 | tf_op jit(solution)/shard_map/reduce_scatter | solution.py:102
  9.7 11.7 %collective-permute-start.1 = (bf16[48,256]{1,0:T(8,128)(2,1)}, bf16[48,256]{1,0:T(8,128)(2,1)}, u32[]{:S(2)}, u32[]{:S(2)}) collective-permute-start(bf16[48,256]{1,0:T(8,128)(2,1)} %get-tuple-element.107), channel_id=1, source_target_pairs={{1,0},{2,1},{3,2},{4,3},{5,4},{6,5},{7,6},{8,7},{9,8},{10,9},{11,1... | collective-permute-start | bytes 73736 | tf_op jit(solution)/shard_map/ppermute | solution.py:18
  11.0 10.4 collective-permute-start
  44.1 961.2 %all-gather.2.cloned.1.call-start = ((), (), s32[]{:S(2)}) async-start(), calls=%async_computation.2 | async-start | bytes 6340608 | tf_op jit(solution)/shard_map/all_gather | solution.py:136
  44.2 654.5 %copy-start.9 = (f32[768]{0:T(1024)S(1)}, f32[768]{0:T(1024)}, u32[]{:S(2)}) copy-start(f32[768]{0:T(1024)} %param.29) | copy-start | bytes 9220
  56.1 644.5 %copy-start.7 = (f32[128]{0:T(128)S(1)}, f32[128]{0:T(128)}, u32[]{:S(2)}) copy-start(f32[128]{0:T(128)} %param.24) | copy-start | bytes 1540
  700.6 422.5 %all-reduce.2.cloned.1.call-start = ((), (), s32[]{:S(2)}) async-start(), calls=%async_computation.3 | async-start | bytes 393216 | tf_op jit(solution)/shard_map/psum | solution.py:155
  700.7 3.0 copy-start.2
  712.5 2.7 copy-start.11
  716.6 3.0 copy-start.2
  728.3 2.7 copy-start.11
  732.4 3.0 copy-start.2
  744.2 2.7 copy-start.11
  748.3 3.0 copy-start.2
  760.0 2.7 copy-start.11
  764.1 3.0 copy-start.2
  775.9 2.7 copy-start.11
  780.0 3.0 copy-start.2
  791.7 2.7 copy-start.11
  795.8 3.0 copy-start.2
  807.6 2.7 copy-start.11
  811.6 3.0 copy-start.2
  823.4 2.7 copy-start.11
  (35 other events, 74.8 us)
Sparse Core Ops, SparseCore 0:
  44.2 652.8 reduce-scatter.1
  700.7 304.4 all-gather.1
  1041.4 81.5 all-reduce.1
where the time goes:
time: 1140 us; the launch traced here: 1130 us
  waiting for transfers between devices  837 us (73%)
  local copies, waits for them, and re-layouts  86 us (8%)
  blocking collectives  79 us (7%)
  matrix products  75.2 us (7%)
  other arithmetic  34.5 us (3%)
  between operations  13.9 us (1%)
    reduce_scatter x1, waiting for transfers between devices, body(): lax.psum_scatter(jnp.dot(onehot, atom_proj, preferred_element_type=jnp.fl...  638 us
    all_gather x1, waiting for transfers between devices, body(): lax.all_gather(token_qkv[:, width_t:], ('row', 'col'), axis=0, tiled=True)  138 us
    psum x1, waiting for transfers between devices, body(): lax.psum(local_numer.astype(jnp.bfloat16), 'col').astype(jnp.float32)  60.5 us
    dynamic_update_slice x24, local copies, waits for them, and re-layouts, body(): lax.map(pair_rows, pair.reshape(query_block // 16, 16, key_block, pair_ch...  44.5 us
    all_gather x1, blocking collectives, body(): queries = lax.all_gather(token_qkv[:, :width_t], 'col', axis=0, tiled=True)  36.4 us
    dot_general x8, matrix products, pair_rows(): jnp.dot(hidden, w_pair_out, preferred_element_type=jnp.float32)  30.4 us
    pmax x1, blocking collectives, body(): largest = lax.pmax(jnp.max(tscores, axis=-1), 'col')  23.5 us
  transfers between devices with their start and end apart: 5, of which 3 were waited for; matrix products, arithmetic and copies ran while one was open for 13% of the time, Pallas kernels for 0%

commit v1 on v0

v1 whole, which is shorter than its diff:
```python
import functools

import jax
import jax.numpy as jnp
from jax import lax
from jax.experimental import pallas as pl
from jax.experimental.pallas import tpu as pltpu
from jax.sharding import PartitionSpec as P

F32, BF16 = jnp.float32, jnp.bfloat16
MESH = pl.DeviceIdType.MESH
NT = (((1,), (1,)), ((), ()))
ROWS, COLS = 16, 8
WINDOW, KEYS, HALO = 32, 128, 48
ATOM_HEADS, TOKEN_HEADS, HEAD = 4, 16, 48
OWN = 16
VMEM_LIMIT = 48 << 20


def dot(a, b):
    return jnp.dot(a, b, preferred_element_type=F32)


def dot_nt(a, b):
    return lax.dot_general(a, b, NT, preferred_element_type=F32)


def remote(src, dst, send, recv, row, col):
    return pltpu.make_async_remote_copy(
        src_ref=src, dst_ref=dst, send_sem=send, recv_sem=recv,
        device_id=(row, col), device_id_type=MESH,
    )


def greet(sem, row, col):
    pl.semaphore_signal(sem, inc=1, device_id=(row, col), device_id_type=MESH)


def atom_attention(x, me, atoms_total, w_qkv, w_out):
    n = 128
    qkv = dot(x, w_qkv).astype(BF16)
    q = qkv[HALO:HALO + n, :128]
    k, v = qkv[:, 128:256], qkv[:, 256:]
    pad = jnp.zeros((256 - k.shape[0], 128), BF16)
    k = jnp.concatenate([k, pad], axis=0)
    v = jnp.concatenate([v, pad], axis=0)
    lane = lax.broadcasted_iota(jnp.int32, (n, 128), 1)
    parts = []
    for h in range(ATOM_HEADS):
        keep = (lane >= 32 * h) & (lane < 32 * h + 32)
        parts.append(jnp.where(keep, q.astype(F32), 0.0).astype(BF16))
    s = dot_nt(jnp.concatenate(parts, axis=0), k) * (32.0 ** -0.5)
    atom = lax.broadcasted_iota(jnp.int32, (n, 256), 0)
    key = lax.broadcasted_iota(jnp.int32, (n, 256), 1)
    first = (atom // WINDOW) * WINDOW
    place = key - HALO + me * n
    shift = jnp.where((place >= 0) & (place < atoms_total), 0.0, -1e9)
    inside = (key >= first) & (key < first + KEYS)
    out = jnp.zeros((n, 128), F32)
    for h in range(ATOM_HEADS):
        sh = jnp.where(inside, s[h * n:(h + 1) * n] + shift, -1e30)
        e = jnp.exp(sh - jnp.max(sh, axis=-1, keepdims=True))
        total = jnp.sum(e, axis=-1, keepdims=True)
        o = dot(e.astype(BF16), v) / total
        keep = (lane >= 32 * h) & (lane < 32 * h + 32)
        out = jnp.where(keep, o, out)
    own = x[HALO:HALO + n].astype(F32)
    return (own + dot(out.astype(BF16), w_out)).astype(BF16)


def tokens_kernel(
    atom_ref, ids_ref, w_aqkv, w_aout, w_agg, gain, w_qkv,
    atom_out_ref, token_ref, q_ref, k_ref, v_ref,
    x_buf, gathered, sums, parts, norm, tq, tk,
    halo_s, halo_r, gat_s, gat_r, sum_s, sum_r, tq_s, tq_r, tk_s, tk_r,
):
    row, col = lax.axis_index("row"), lax.axis_index("col")
    me = row * COLS + col
    left, right = (me + 127) % 128, (me + 1) % 128
    key_col = row // 2
    mine = (key_col == col).astype(jnp.int32)

    barrier = pltpu.get_barrier_semaphore()
    greet(barrier, left // COLS, left % COLS)
    greet(barrier, right // COLS, right % COLS)
    for d in range(1, ROWS):
        greet(barrier, (row + d) % ROWS, col)
    for d in range(1, COLS):
        greet(barrier, row, (col + d) % COLS)
    for s in range(16):
        r2, c2 = 2 * col + s // COLS, s % COLS

        @pl.when((r2 != row) | (c2 != col))
        def _():
            greet(barrier, r2, c2)

    x_buf[HALO:HALO + 128] = atom_ref[...]
    pl.semaphore_wait(barrier, 2 + 15 + 7 + 16 - mine)

    to_right = remote(atom_ref.at[pl.ds(80, 48)], x_buf.at[pl.ds(0, 48)],
                      halo_s.at[0], halo_r.at[0], right // COLS, right % COLS)
    to_left = remote(atom_ref.at[pl.ds(0, 48)], x_buf.at[pl.ds(176, 48)],
                     halo_s.at[1], halo_r.at[1], left // COLS, left % COLS)
    to_right.start()
    to_left.start()

    own_tokens = me * OWN + lax.broadcasted_iota(jnp.int32, (OWN, 128), 0)

    def count_step(i, acc):
        ids = ids_ref[pl.ds(i * 8, 8), :]
        for t in range(8):
            acc = acc + (own_tokens == ids[t:t + 1]).astype(F32)
        return acc

    counts = lax.fori_loop(0, 16, count_step, jnp.zeros((OWN, 128), F32))
    count = jnp.sum(counts, axis=-1, keepdims=True)
    to_right.wait()
    to_left.wait()

    atom_out = atom_attention(x_buf[...], me, 128 * 128, w_aqkv[...], w_aout[...])
    atom_out_ref[...] = atom_out
    gathered[pl.ds(row, 1)] = atom_out[None]

    def gather(d):
        return remote(gathered.at[row], gathered.at[row], gat_s.at[d], gat_r.at[row],
                      (row + d) % ROWS, col)

    def gather_in(d):
        j = (row + d) % ROWS
        return remote(gathered.at[j], gathered.at[j], gat_s.at[d], gat_r.at[j], row, col)

    for d in range(1, ROWS):
        gather(d).start()
    for d in range(1, ROWS):
        gather_in(d).wait_recv()

    token = row * 128 + lax.broadcasted_iota(jnp.int32, (128, 128), 0)
    total = jnp.zeros((128, 768), F32)
    for j in range(0, ROWS, 2):
        a = jnp.concatenate([gathered[j], gathered[j + 1]], axis=0)
        proj = jnp.maximum(dot(a, w_agg[...]), 0.0).astype(BF16)
        hot = [
            (token == ids_ref[pl.ds(COLS * (j + t) + col, 1), :]).astype(F32).astype(BF16)
            for t in range(2)
        ]
        total = total + dot(jnp.concatenate(hot, axis=1), proj)
    sums[...] = total.reshape(COLS, OWN, 768)

    def send_sum(d):
        c2 = (col + d) % COLS
        return remote(sums.at[c2], parts.at[col], sum_s.at[d], sum_r.at[col], row, c2)

    def recv_sum(d):
        c2 = (col + d) % COLS
        return remote(sums.at[c2], parts.at[c2], sum_s.at[d], sum_r.at[c2], row, col)

    for d in range(1, COLS):
        send_sum(d).start()
    parts[pl.ds(col, 1)] = sums[pl.ds(col, 1)]
    for d in range(1, COLS):
        recv_sum(d).wait_recv()
    acc = parts[0]
    for s in range(1, COLS):
        acc = acc + parts[s]
    token_in = (acc / count).astype(BF16)
    token_ref[...] = token_in
    t = token_in.astype(F32)
    tc = t - jnp.mean(t, axis=-1, keepdims=True)
    var = jnp.mean(tc * tc, axis=-1, keepdims=True)
    norm[...] = (tc * lax.rsqrt(var + 1e-5) * gain[...]).astype(BF16)
    tq[pl.ds(col, 1)] = norm[...][None]
    slot = COLS * (row % 2) + col

    def send_q(d):
        return remote(norm, tq.at[col], tq_s.at[d], tq_r.at[col], row, (col + d) % COLS)

    def recv_q(d):
        c2 = (col + d) % COLS
        return remote(norm, tq.at[c2], tq_s.at[d], tq_r.at[c2], row, col)

    def send_k(d):
        return remote(norm, tk.at[slot], tk_s.at[d], tk_r.at[slot], (row + d) % ROWS, key_col)

    def recv_k(s):
        return remote(norm, tk.at[s], tk_s.at[s], tk_r.at[s], row, col)

    for d in range(1, ROWS):
        send_k(d).start()

    @pl.when(mine == 0)
    def _():
        send_k(0).start()

    @pl.when(mine == 1)
    def _():
        tk[pl.ds(slot, 1)] = norm[...][None]

    for d in range(1, COLS):
        send_q(d).start()
    for d in range(1, COLS):
        recv_q(d).wait_recv()
    tqv = tq[...].reshape(128, 768)
    q_ref[...] = dot(tqv, w_qkv[:, :768]).astype(BF16)
    for s in range(16):
        @pl.when((2 * col + s // COLS != row) | (s % COLS != col))
        def _():
            recv_k(s).wait_recv()

    tkv = tk[...].reshape(256, 768)
    k_ref[...] = dot(tkv, w_qkv[:, 768:1536]).astype(BF16)
    v_ref[...] = dot(tkv, w_qkv[:, 1536:]).astype(BF16)

    for d in range(1, ROWS):
        gather(d).wait_send()
        send_k(d).wait_send()
    for d in range(1, COLS):
        send_sum(d).wait_send()
        send_q(d).wait_send()

    @pl.when(mine == 0)
    def _():
        send_k(0).wait_send()


def norm_rows(x_bf, gain, ones):
    x = x_bf.astype(F32)
    xc = x - dot(x_bf, ones)
    var = jnp.mean(xc * xc, axis=-1, keepdims=True)
    return x, (xc * lax.rsqrt(var + 1e-5) * gain).astype(BF16)


def pair_kernel(x_ref, w_in, w_out, w_bias, g_pair, g_bias, ones, out_ref, bias_ref):
    n, keys, chan = x_ref.shape
    x, normed = norm_rows(x_ref[...].reshape(n * keys, chan), g_pair[...], ones[...])
    both = dot(normed, w_in[...])
    half, up = both[:, :256], both[:, 256:]
    hidden = ((half + half * jnp.tanh(half)) * up).astype(BF16)
    new = (x + dot(hidden, w_out[...])).astype(BF16)
    out_ref[...] = new.reshape(n, keys, chan)
    _, normed = norm_rows(new, g_bias[...], ones[...])
    for t in range(n):
        bias_ref[16 * t:16 * t + 16, :] = dot_nt(w_bias[...], normed[t * keys:(t + 1) * keys])


def pair_step(pair, w_in, w_out, w_bias, g_pair, g_bias):
    nq, keys, chan = pair.shape
    block = 16
    hidden = w_out.shape[0]
    w_in = jnp.concatenate([w_in[:, :hidden] * jnp.asarray(0.5, BF16), w_in[:, hidden:]], axis=1)
    ones = jnp.full((chan, chan), 1.0 / chan, BF16)

    def whole(a):
        return pl.BlockSpec(a.shape, lambda i: (0,) * a.ndim)

    weights = (w_in, w_out, w_bias.T, g_pair.reshape(1, chan), g_bias.reshape(1, chan), ones)
    return pl.pallas_call(
        pair_kernel,
        grid=(nq // block,),
        in_specs=[pl.BlockSpec((block, keys, chan), lambda i: (i, 0, 0))] + [whole(a) for a in weights],
        out_specs=[
            pl.BlockSpec((block, keys, chan), lambda i: (i, 0, 0)),
            pl.BlockSpec((block * 16, keys), lambda i: (i, 0)),
        ],
        out_shape=[
            jax.ShapeDtypeStruct(pair.shape, BF16),
            jax.ShapeDtypeStruct((nq * 16, keys), F32),
        ],
        compiler_params=pltpu.CompilerParams(vmem_limit_bytes=VMEM_LIMIT),
        name="pair",
    )(pair, *weights)


def attend_kernel(
    q_ref, k_ref, v_ref, bias_ref, mask_ref, w_out, token_ref,
    out_ref,
    num_out, st_out, num_in, st_in, num_s, num_r, st_s, st_r,
):
    row, col = lax.axis_index("row"), lax.axis_index("col")
    barrier = pltpu.get_barrier_semaphore()
    for d in range(1, COLS):
        greet(barrier, row, (col + d) % COLS)

    head = lax.broadcasted_iota(jnp.int32, (16, 768), 0)
    lane = lax.broadcasted_iota(jnp.int32, (16, 768), 1)
    heads = jnp.where((lane >= head * HEAD) & (lane < head * HEAD + HEAD), 1.0, 0.0)
    eye = jnp.where(
        lax.broadcasted_iota(jnp.int32, (16, 128), 0) == lax.broadcasted_iota(jnp.int32, (16, 128), 1),
        1.0, 0.0,
    )
    masking = (mask_ref[...].astype(F32) - 1.0) * 1e9

    def chunk(c2):
        qs = q_ref[pl.ds(c2 * OWN, OWN), :].astype(F32)
        big = (qs[:, None, :] * heads[None]).reshape(256, 768).astype(BF16)
        s = dot_nt(big, k_ref[...]) * (HEAD ** -0.5)
        s = s + bias_ref[pl.ds(c2 * 256, 256), :] + masking
        top = jnp.max(s, axis=-1, keepdims=True)
        e = jnp.exp(s - top)
        total = jnp.sum(e, axis=-1, keepdims=True)
        o = dot(e.astype(BF16), v_ref[...])
        num = jnp.sum(o.reshape(OWN, 16, 768) * heads[None], axis=1)
        tops = jnp.sum(jnp.broadcast_to(top, (256, 128)).reshape(OWN, 16, 128) * eye[None], axis=1)
        totals = jnp.sum(jnp.broadcast_to(total, (256, 128)).reshape(OWN, 16, 128) * eye[None], axis=1)
        return num.astype(BF16), jnp.concatenate([tops, totals], axis=0)

    def send(d):
        c2 = (col + d) % COLS
        return (
            remote(num_out.at[c2], num_in.at[col], num_s.at[d], num_r.at[col], row, c2),
            remote(st_out.at[c2], st_in.at[col], st_s.at[d], st_r.at[col], row, c2),
        )

    def receive(d):
        c2 = (col + d) % COLS
        return (
            remote(num_out.at[c2], num_in.at[c2], num_s.at[d], num_r.at[c2], row, col),
            remote(st_out.at[c2], st_in.at[c2], st_s.at[d], st_r.at[c2], row, col),
        )

    for d in range(1, COLS):
        c2 = (col + d) % COLS
        num, st = chunk(c2)
        num_out[pl.ds(c2, 1)] = num[None]
        st_out[pl.ds(c2, 1)] = st[None]
        if d == 1:
            pl.semaphore_wait(barrier, COLS - 1)
        for copy in send(d):
            copy.start()
    num, st = chunk(col)
    num_in[pl.ds(col, 1)] = num[None]
    st_in[pl.ds(col, 1)] = st[None]
    for d in range(1, COLS):
        for copy in receive(d):
            copy.wait_recv()
    st = st_in[...]
    tops, totals = st[:, :OWN], st[:, OWN:]
    best = jnp.max(tops, axis=0, keepdims=True)
    w = jnp.exp(tops - best)
    den = jnp.sum(w * totals, axis=0)
    small = jnp.concatenate([w.reshape(COLS * OWN, 128), den], axis=0)
    wide = jnp.concatenate([heads, jnp.zeros((112, 768), F32)], axis=0)
    spread = jnp.dot(small, wide, preferred_element_type=F32, precision=lax.Precision.HIGHEST)
    num = jnp.zeros((OWN, 768), F32)
    for s in range(COLS):
        num = num + num_in[s].astype(F32) * spread[s * OWN:(s + 1) * OWN]
    mix = (num / spread[COLS * OWN:]).astype(BF16)
    out_ref[...] = (token_ref[...].astype(F32) + dot(mix, w_out[...])).astype(BF16)
    for d in range(1, COLS):
        for copy in send(d):
            copy.wait_send()


def body(
    atom_single, atom_to_token, token_mask, pair, w_atom_qkv, w_atom_out, w_aggregate,
    pair_gain, w_pair_in, w_pair_out, bias_gain, w_bias, token_gain, w_token_qkv, w_token_out,
):
    vmem = pl.BlockSpec(memory_space=pltpu.VMEM)
    dma = pltpu.SemaphoreType.DMA
    atom_out, token_in, q, k, v = pl.pallas_call(
        tokens_kernel,
        in_specs=[vmem] * 7,
        out_specs=[vmem] * 5,
        out_shape=[
            jax.ShapeDtypeStruct((128, 128), BF16),
            jax.ShapeDtypeStruct((OWN, 768), BF16),
            jax.ShapeDtypeStruct((128, 768), BF16),
            jax.ShapeDtypeStruct((256, 768), BF16),
            jax.ShapeDtypeStruct((256, 768), BF16),
        ],
        scratch_shapes=[
            pltpu.VMEM((224, 128), BF16),
            pltpu.VMEM((ROWS, 128, 128), BF16),
            pltpu.VMEM((COLS, OWN, 768), F32),
            pltpu.VMEM((COLS, OWN, 768), F32),
            pltpu.VMEM((OWN, 768), BF16),
            pltpu.VMEM((COLS, OWN, 768), BF16),
            pltpu.VMEM((16, OWN, 768), BF16),
            dma((2,)), dma((2,)), dma((ROWS,)), dma((ROWS,)), dma((COLS,)), dma((COLS,)),
            dma((COLS,)), dma((COLS,)), dma((16,)), dma((16,)),
        ],
        compiler_params=pltpu.CompilerParams(
            collective_id=0, has_side_effects=True, vmem_limit_bytes=VMEM_LIMIT
        ),
        name="tokens",
    )(
        atom_single, atom_to_token.reshape(128, 128), w_atom_qkv, w_atom_out, w_aggregate,
        token_gain.reshape(1, 768), w_token_qkv,
    )
    pair_out, bias = pair_step(pair, w_pair_in, w_pair_out, w_bias, pair_gain, bias_gain)
    token_out = pl.pallas_call(
        attend_kernel,
        in_specs=[vmem] * 7,
        out_specs=vmem,
        out_shape=jax.ShapeDtypeStruct((OWN, 768), BF16),
        scratch_shapes=[
            pltpu.VMEM((COLS, OWN, 768), BF16),
            pltpu.VMEM((COLS, 2 * OWN, 128), F32),
            pltpu.VMEM((COLS, OWN, 768), BF16),
            pltpu.VMEM((COLS, 2 * OWN, 128), F32),
            dma((COLS,)), dma((COLS,)), dma((COLS,)), dma((COLS,)),
        ],
        compiler_params=pltpu.CompilerParams(
            collective_id=1, has_side_effects=True, vmem_limit_bytes=VMEM_LIMIT
        ),
        name="attend",
    )(q, k, v, bias, token_mask.reshape(1, 256), w_token_out, token_in)
    return (atom_out, token_out, pair_out)


def solution(mesh):
    atoms = P(("row", "col"), None)
    pairs = P("row", "col", None)
    return jax.shard_map(
        body,
        mesh=mesh,
        in_specs=(atoms, P(), P("col"), pairs) + (P(),) * 11,
        out_specs=(atoms, atoms, pairs),
        check_vma=False,
    )
```

time: 1140 us -> 103 us (0.09)
  waiting for transfers between devices: 837 us -> 0 us
  Pallas kernels: 0 us -> 92.5 us
  blocking collectives: 79 us -> 0 us
  local copies, waits for them, and re-layouts: 86 us -> 8.16 us
  matrix products: 75.2 us -> 0 us
  other arithmetic: 34.5 us -> 0.89 us
  between operations: 13.9 us -> 0.76 us
    reduce_scatter x1 -> x0, waiting for transfers between devices: 638 us -> none  [body(): lax.psum_scatter(jnp.dot(onehot, atom_proj, preferred_element_type=jnp.fl...]
    all_gather x1 -> x0, waiting for transfers between devices: 138 us -> none  [body(): lax.all_gather(token_qkv[:, width_t:], ('row', 'col'), axis=0, tiled=True)]
    pallas_call x0 -> x3, Pallas kernels: none -> 92.5 us  [the longest x1 54.3 us: body(): pl.pallas_call(tokens_kernel, in_specs=[vmem] * 7, out_specs=[vmem] * 5,...]
    dot_general x33 -> x0, matrix products: 75.2 us -> none  [the longest x8 30.4 us: pair_rows(): jnp.dot(hidden, w_pair_out, preferred_element_type=jnp.float32)]
    psum x1 -> x0, waiting for transfers between devices: 60.5 us -> none  [body(): lax.psum(local_numer.astype(jnp.bfloat16), 'col').astype(jnp.float32)]
    dynamic_update_slice x24 -> x0, local copies, waits for them, and re-layouts: 44.5 us -> none  [body(): lax.map(pair_rows, pair.reshape(query_block // 16, 16, key_block, pair_ch...]
    all_gather x1 -> x0, blocking collectives: 36.4 us -> none  [body(): queries = lax.all_gather(token_qkv[:, :width_t], 'col', axis=0, tiled=True)]
    reduce_sum x29 -> x0, other arithmetic: 30.9 us -> none  [the longest x17 14.9 us: layer_norm(): var = jnp.mean((x - mean) ** 2, axis=-1, keepdims=True)]
  transfers between devices with their start and end apart: 5 -> 0, of which waited for: 3 -> 0; matrix products, arithmetic and copies ran while one was open for 13% -> 0% of each run, Pallas kernels for 0% -> 0%
where the time goes in v1:
time: 103 us; the launch traced here: 102 us
  Pallas kernels  92.5 us (90%)
  local copies, waits for them, and re-layouts  8.16 us (8%)
    pallas_call x1, Pallas kernels, body(): pl.pallas_call(tokens_kernel, in_specs=[vmem] * 7, out_specs=[vmem] * 5,...  54.3 us
    pallas_call x1, Pallas kernels, pair_step(): pl.pallas_call(pair_kernel, grid=(nq // block,), in_specs=[pl.BlockSpec((...  25.7 us
    pallas_call x1, Pallas kernels, body(): pl.pallas_call(attend_kernel, in_specs=[vmem] * 7, out_specs=vmem, out_sh...  12.6 us
    unnamed x26, local copies, waits for them, and re-layouts  7.42 us

profile of v1, /device:TPU:0, one launch (start us, length us, event | category | flops | bytes accessed | tf_op | source)
XLA Modules:
  0.0 102.4 jit_solution(4978739784717262407)
XLA Ops:
  0.6 0.0 copy-start.8
  0.6 0.0 copy-start.11
  0.7 0.0 copy-start.5
  0.7 0.0 copy-start.10
  0.7 0.7 reshape.22.gain
  1.4 0.9 slice_multiply_fusion
  2.3 0.0 copy-start
  2.3 2.0 %copy-done = bf16[768,2304]{1,0:T(8,128)(2,1)S(1)} copy-done((bf16[768,2304]{1,0:T(8,128)(2,1)S(1)}, bf16[768,2304]{1,0:T(8,128)(2,1)}, u32[]{:S(2)}) %copy-start) | copy-done | bytes 3538968
  4.3 0.9 copy-done.2
  5.2 0.9 copy-done.3
  6.1 0.8 copy-done.4
  7.0 0.8 copy-done.6
  7.7 0.8 copy-done.7
  8.5 54.3 %tokens.1 = (bf16[128,128]{1,0:T(8,128)(2,1)S(1)}, bf16[16,768]{1,0:T(8,128)(2,1)S(1)}, bf16[128,768]{1,0:T(8,128)(2,1)S(1)}, bf16[256,768]{1,0:T(8,128)(2,1)S(1)}, bf16[256,768]{1,0:T(8,128)(2,1)S(1)}) custom-call(bf16[128,128]{1,0:T(8,128)(2,1)S(1)} %copy-done.6, s32[128,128]{1,0:T(8,128)S(1)} %bitcast.5, bf16[128,384]{1,0:T(8,128)(2,1)S(1)} %copy-done.3, ...), custom_call_target="tpu_custom_call" | custom-call | tf_op jit(solution)/shard_map/tokens/pallas_call | solution.py:359
  62.8 0.0 copy-done.8
  62.8 0.0 copy-done.11
  62.8 0.0 copy-done.5
  62.8 0.0 copy-done.10
  62.9 0.0 copy-start.1
  62.9 0.0 copy-start.9
  62.9 25.7 %pair.1 = (bf16[128,256,128]{2,1,0:T(8,128)(2,1)}, f32[2048,256]{1,0:T(8,128)S(1)}) custom-call(bf16[128,256,128]{2,1,0:T(8,128)(2,1)} %x_ref.1, bf16[128,512]{1,0:T(8,128)(2,1)S(1)} %pad_maximum_fusion.w_in, bf16[256,128]{1,0:T(8,128)(2,1)S(1)} %copy-done.5, bf16[16,128]{1,0:T(8,128)(2,1)S(1)} %bitcast.6, f32[1,128]{1,0:T(1,128)S(1)} %bitcast.8, ...), custom_call_target="tpu_custom_call" | custom-call | tf_op jit(solution)/shard_map/pair/pallas_call | solution.py:256
  88.5 12.6 %attend.1 = bf16[16,768]{1,0:T(8,128)(2,1)S(1)} custom-call(bf16[128,768]{1,0:T(8,128)(2,1)S(1)} %get-tuple-element.11.q_ref, bf16[256,768]{1,0:T(8,128)(2,1)S(1)} %get-tuple-element.12.k_ref, bf16[256,768]{1,0:T(8,128)(2,1)S(1)} %get-tuple-element.13.v_ref, f32[2048,256]{1,0:T(8,128)S(1)} %get-tuple-element.14.bias_ref, s32[1,256]{1,0:T(1,128)S(1)} %bitcast.7, ...), custom_call_target="tpu_custom_call" | custom-call | tf_op jit(solution)/shard_map/attend/pallas_call | solution.py:390
  101.1 0.6 copy.20
  101.7 0.6 copy.21
  (9 shorter events, 0.0 us)
Async XLA Ops:
  0.6 62.2 %copy-start.8 = (bf16[128,16]{0,1:T(8,128)(2,1)S(1)}, bf16[128,16]{0,1:T(8,128)(2,1)}, u32[]{:S(2)}) copy-start(bf16[128,16]{0,1:T(8,128)(2,1)} %param.26) | copy-start | bytes 12292
  0.6 62.2 %copy-start.11 = (f32[128]{0:T(128)S(1)}, f32[128]{0:T(128)}, u32[]{:S(2)}) copy-start(f32[128]{0:T(128)} %param.25) | copy-start | bytes 1540
  0.7 62.2 %copy-start.5 = (bf16[256,128]{1,0:T(8,128)(2,1)S(1)}, bf16[256,128]{1,0:T(8,128)(2,1)}, u32[]{:S(2)}) copy-start(bf16[256,128]{1,0:T(8,128)(2,1)} %w_out.2) | copy-start | bytes 196612
  0.7 62.2 %copy-start.10 = (f32[128]{0:T(128)S(1)}, f32[128]{0:T(128)}, u32[]{:S(2)}) copy-start(f32[128]{0:T(128)} %param.22) | copy-start | bytes 1540
  2.3 2.0 %copy-start = (bf16[768,2304]{1,0:T(8,128)(2,1)S(1)}, bf16[768,2304]{1,0:T(8,128)(2,1)}, u32[]{:S(2)}) copy-start(bf16[768,2304]{1,0:T(8,128)(2,1)} %w_qkv.1) | copy-start | bytes 10616836
  4.3 0.9 copy-start.2
  5.2 0.9 copy-start.3
  6.1 0.8 copy-start.4
  7.0 0.8 copy-start.6
  7.7 0.8 copy-start.7
  62.9 25.7 %copy-start.1 = (bf16[768,768]{1,0:T(8,128)(2,1)S(1)}, bf16[768,768]{1,0:T(8,128)(2,1)}, u32[]{:S(2)}) copy-start(bf16[768,768]{1,0:T(8,128)(2,1)} %w_out.3) | copy-start | bytes 3538948
  62.9 25.7 %copy-start.9 = (s32[256]{0:T(256)S(1)}, s32[256]{0:T(256)}, u32[]{:S(2)}) copy-start(s32[256]{0:T(256)} %param.17) | copy-start | bytes 3076

commit v2 on v1

v2 whole, which is shorter than its diff:
```python
import functools

import jax
import jax.numpy as jnp
from jax import lax
from jax.experimental import pallas as pl
from jax.experimental.pallas import tpu as pltpu
from jax.sharding import PartitionSpec as P

F32, BF16 = jnp.float32, jnp.bfloat16
MESH = pl.DeviceIdType.MESH
NT = (((1,), (1,)), ((), ()))
ROWS, COLS = 16, 8
WINDOW, KEYS, HALO = 32, 128, 48
ATOM_HEADS, TOKEN_HEADS, HEAD = 4, 16, 48
OWN = 16
VMEM_LIMIT = 56 << 20
SUM_TYPE = BF16
CHUNK = 16
EARLY = 7
STAGES = (0, 1, 3, 4, 5)


def dot(a, b):
    return jnp.dot(a, b, preferred_element_type=F32)


def dot_nt(a, b):
    return lax.dot_general(a, b, NT, preferred_element_type=F32)


def remote(src, dst, send, recv, row, col):
    return pltpu.make_async_remote_copy(
        src_ref=src, dst_ref=dst, send_sem=send, recv_sem=recv,
        device_id=(row, col), device_id_type=MESH,
    )


def greet(sem, row, col):
    pl.semaphore_signal(sem, inc=1, device_id=(row, col), device_id_type=MESH)


def atom_attention(x, me, atoms_total, w_qkv, w_out):
    n = 128
    qkv = dot(x, w_qkv).astype(BF16)
    q = qkv[HALO:HALO + n, :128]
    k, v = qkv[:, 128:256], qkv[:, 256:]
    pad = jnp.zeros((256 - k.shape[0], 128), BF16)
    k = jnp.concatenate([k, pad], axis=0)
    v = jnp.concatenate([v, pad], axis=0)
    lane = lax.broadcasted_iota(jnp.int32, (n, 128), 1)
    parts = []
    for h in range(ATOM_HEADS):
        keep = (lane >= 32 * h) & (lane < 32 * h + 32)
        parts.append(jnp.where(keep, q.astype(F32), 0.0).astype(BF16))
    s = dot_nt(jnp.concatenate(parts, axis=0), k) * (32.0 ** -0.5)
    atom = lax.broadcasted_iota(jnp.int32, (n, 256), 0)
    key = lax.broadcasted_iota(jnp.int32, (n, 256), 1)
    first = (atom // WINDOW) * WINDOW
    place = key - HALO + me * n
    shift = jnp.where((place >= 0) & (place < atoms_total), 0.0, -1e9)
    inside = (key >= first) & (key < first + KEYS)
    out = jnp.zeros((n, 128), F32)
    for h in range(ATOM_HEADS):
        sh = jnp.where(inside, s[h * n:(h + 1) * n] + shift, -1e30)
        e = jnp.exp(sh - jnp.max(sh, axis=-1, keepdims=True))
        total = jnp.sum(e, axis=-1, keepdims=True)
        o = dot(e.astype(BF16), v) / total
        keep = (lane >= 32 * h) & (lane < 32 * h + 32)
        out = jnp.where(keep, o, out)
    own = x[HALO:HALO + n].astype(F32)
    return (own + dot(out.astype(BF16), w_out)).astype(BF16)


def norm_rows(x_bf, gain, ones):
    x = x_bf.astype(F32)
    xc = x - dot(x_bf, ones)
    var = jnp.mean(xc * xc, axis=-1, keepdims=True)
    return x, (xc * lax.rsqrt(var + 1e-5) * gain).astype(BF16)


def pair_weights(w_in, half_in, ones):
    half_in[:, :256] = w_in[:, :256] * jnp.asarray(0.5, BF16)
    half_in[:, 256:] = w_in[:, 256:]
    ones[...] = jnp.full(ones.shape, 1.0 / 128.0, BF16)


def pair_chunk(x, w_in, w_out, bias_t, g_pair, g_bias, ones, put_bias):
    n, keys, chan = x.shape
    x, normed = norm_rows(x.reshape(n * keys, chan), g_pair[...], ones[...])
    both = dot(normed, w_in[...])
    half, up = both[:, :256], both[:, 256:]
    hidden = ((half + half * jnp.tanh(half)) * up).astype(BF16)
    new = (x + dot(hidden, w_out[...])).astype(BF16)
    _, normed = norm_rows(new, g_bias[...], ones[...])
    for t in range(n):
        put_bias(t, dot_nt(bias_t[...], normed[t * keys:(t + 1) * keys]))
    return new.reshape(n, keys, chan)


def token_norm(t, gain):
    gain = jnp.concatenate([gain[i:i + 1] for i in range(6)], axis=1)
    t = t.astype(F32)
    tc = t - jnp.mean(t, axis=-1, keepdims=True)
    var = jnp.mean(tc * tc, axis=-1, keepdims=True)
    return (tc * lax.rsqrt(var + 1e-5) * gain).astype(BF16)


def tokens_kernel(
    atom_hbm, ids_hbm, w_aqkv_hbm, w_aout_hbm, w_agg_hbm, gain_hbm, w_qkv_hbm,
    pair_hbm, w_in_hbm, w_out_hbm, bias_t_hbm, g_pair_hbm, g_bias_hbm,
    atom_out_ref, token_ref, q_ref, k_ref, v_ref, pair_out_hbm, bias_ref,
    atom, ids, w_aqkv, w_aout, w_agg, gain, w_qkv, w_in, w_out, bias_t, g_pair, g_bias,
    half_in, ones, pair_in, pair_new,
    x_buf, gathered, sums, parts, counts, key_token, own_token, key_norm, own_norm, tq, tk,
    load, pair_r, pair_w,
    halo_s, halo_r, gat_s, gat_r, sum_s, sum_r, move_s, move_r, tq_s, tq_r, tk_s, tk_r,
):
    row, col = lax.axis_index("row"), lax.axis_index("col")
    me = row * COLS + col
    left, right = (me + 127) % 128, (me + 1) % 128
    to_row, to_col = 2 * col + row // COLS, row % COLS
    from_row, from_col = COLS * (row % 2) + col, row // 2
    stays = ((to_row == row) & (to_col == col)).astype(jnp.int32)

    barrier = pltpu.get_barrier_semaphore()
    greet(barrier, left // COLS, left % COLS)
    greet(barrier, right // COLS, right % COLS)
    for d in range(1, ROWS):
        greet(barrier, (row + d) % ROWS, col)
    for d in range(1, COLS):
        greet(barrier, row, (col + d) % COLS)

    @pl.when(stays == 0)
    def _():
        greet(barrier, from_row, from_col)

    pairs = [
        (w_in_hbm, w_in), (w_out_hbm, w_out), (bias_t_hbm, bias_t), (g_pair_hbm, g_pair),
        (g_bias_hbm, g_bias), (atom_hbm, atom), (ids_hbm, ids), (w_aqkv_hbm, w_aqkv),
        (w_aout_hbm, w_aout), (w_agg_hbm, w_agg), (gain_hbm, gain), (w_qkv_hbm, w_qkv),
    ]
    loads = [pltpu.make_async_copy(a, b, load.at[i]) for i, (a, b) in enumerate(pairs)]
    chunks = pair_in.shape[0]

    def read(i):
        return pltpu.make_async_copy(
            pair_hbm.at[pl.ds(i * CHUNK, CHUNK)], pair_in.at[i], pair_r.at[i])

    def write(i):
        return pltpu.make_async_copy(
            pair_new.at[i], pair_out_hbm.at[pl.ds(i * CHUNK, CHUNK)], pair_w.at[i])

    for copy in loads[:5]:
        copy.start()
    read(0).start()
    for copy in loads[5:]:
        copy.start()
    for i in range(1, chunks):
        read(i).start()
    for copy in loads[:5]:
        copy.wait()
    pair_weights(w_in, half_in, ones)
    for copy in loads[5:]:
        copy.wait()
    x_buf[HALO:HALO + 128] = atom[...]

    to_right = remote(atom.at[pl.ds(80, 48)], x_buf.at[pl.ds(0, 48)],
                      halo_s.at[0], halo_r.at[0], right // COLS, right % COLS)
    to_left = remote(atom.at[pl.ds(0, 48)], x_buf.at[pl.ds(176, 48)],
                     halo_s.at[1], halo_r.at[1], left // COLS, left % COLS)

    def gather(d):
        return remote(gathered.at[row], gathered.at[row], gat_s.at[d], gat_r.at[row],
                      (row + d) % ROWS, col)

    def gather_in(d):
        j = (row + d) % ROWS
        return remote(gathered.at[j], gathered.at[j], gat_s.at[d], gat_r.at[j], row, col)

    def send_sum(d):
        c2 = (col + d) % COLS
        return remote(sums.at[c2], parts.at[col], sum_s.at[d], sum_r.at[col], row, c2)

    def recv_sum(d):
        c2 = (col + d) % COLS
        return remote(sums.at[c2], parts.at[c2], sum_s.at[d], sum_r.at[c2], row, col)

    move = remote(key_token, own_token, move_s.at[0], move_r.at[0], to_row, to_col)

    def send_q(d):
        return remote(own_norm, tq.at[col], tq_s.at[d], tq_r.at[col], row, (col + d) % COLS)

    def recv_q(d):
        c2 = (col + d) % COLS
        return remote(own_norm, tq.at[c2], tq_s.at[d], tq_r.at[c2], row, col)

    def send_k(d):
        return remote(key_norm, tk.at[row], tk_s.at[d], tk_r.at[row], (row + d) % ROWS, col)

    def recv_k(d):
        r2 = (row + d) % ROWS
        return remote(key_norm, tk.at[r2], tk_s.at[d], tk_r.at[r2], row, col)

    def start_halo():
        pl.semaphore_wait(barrier, 2 + 15 + 7 + 1 - stays)
        to_right.start()
        to_left.start()
        own_tokens = col * 256 + row * OWN + lax.broadcasted_iota(jnp.int32, (OWN, 128), 0)
        acc = jnp.zeros((OWN, 128), F32)
        for t in range(128):
            acc = acc + (own_tokens == ids[t:t + 1, :]).astype(F32)
        counts[...] = jnp.broadcast_to(jnp.sum(acc, axis=-1, keepdims=True), (OWN, 128))

    def start_gather():
        to_right.wait()
        to_left.wait()
        atom_out = atom_attention(x_buf[...], me, 128 * 128, w_aqkv[...], w_aout[...])
        atom_out_ref[...] = atom_out
        gathered[pl.ds(row, 1)] = atom_out[None]
        for d in range(1, ROWS):
            gather(d).start()

    def start_sums():
        for d in range(1, ROWS):
            gather_in(d).wait_recv()
        place = lax.broadcasted_iota(jnp.int32, (128, 128), 0)
        token = (place // OWN) * 256 + row * OWN + place % OWN
        total = jnp.zeros((128, 768), F32)
        for j in range(0, ROWS, 2):
            a = jnp.concatenate([gathered[j], gathered[j + 1]], axis=0)
            proj = jnp.maximum(dot(a, w_agg[...]), 0.0).astype(BF16)
            hot = [
                (token == ids[pl.ds(COLS * (j + t) + col, 1), :]).astype(F32).astype(BF16)
                for t in range(2)
            ]
            total = total + dot(jnp.concatenate(hot, axis=1), proj)
        sums[...] = total.astype(sums.dtype).reshape(COLS, OWN, 768)
        for d in range(1, COLS):
            send_sum(d).start()
        parts[pl.ds(col, 1)] = sums[pl.ds(col, 1)]

    def start_keys():
        for d in range(1, COLS):
            recv_sum(d).wait_recv()
        acc = parts[0].astype(F32)
        for s in range(1, COLS):
            acc = acc + parts[s].astype(F32)
        token_in = (acc / counts[:, :1]).astype(BF16)
        key_token[...] = token_in

        @pl.when(stays == 0)
        def _():
            move.start()

        @pl.when(stays == 1)
        def _():
            own_token[...] = token_in

        key_norm[...] = token_norm(token_in, gain[...])
        tk[pl.ds(row, 1)] = key_norm[...][None]
        for d in range(1, ROWS):
            send_k(d).start()

    def start_queries():
        @pl.when(stays == 0)
        def _():
            move.wait()

        token_ref[...] = own_token[...]
        own_norm[...] = token_norm(own_token[...], gain[...])
        tq[pl.ds(col, 1)] = own_norm[...][None]
        for d in range(1, COLS):
            send_q(d).start()

    def step(i, carry):
        read(i).wait()

        def put_bias(t, b):
            bias_ref[pl.ds(pl.multiple_of(i * CHUNK * 16 + 16 * t, 16), 16), :] = b

        pair_new[i] = pair_chunk(pair_in[i], half_in, w_out, bias_t, g_pair, g_bias, ones, put_bias)
        write(i).start()
        for at, stage in zip(STAGES, (start_halo, start_gather, start_sums, start_keys, start_queries)):
            pl.when(i == at)(stage)
        return carry

    lax.fori_loop(0, chunks, step, 0)

    for d in range(1, COLS):
        recv_q(d).wait_recv()
    tqv = tq[...].reshape(128, 768)
    q_ref[...] = dot(tqv, w_qkv[:, :768]).astype(BF16)
    for d in range(1, ROWS):
        recv_k(d).wait_recv()
    tkv = tk[...].reshape(256, 768)
    k_ref[...] = dot(tkv, w_qkv[:, 768:1536]).astype(BF16)
    v_ref[...] = dot(tkv, w_qkv[:, 1536:]).astype(BF16)

    for d in range(1, ROWS):
        gather(d).wait_send()
        send_k(d).wait_send()
    for d in range(1, COLS):
        send_sum(d).wait_send()
        send_q(d).wait_send()
    for i in range(chunks):
        write(i).wait()


def rest_kernel(
    pair_hbm, done_hbm, w_in, w_out, bias_t, g_pair, g_bias,
    out_hbm, bias_ref,
    half_in, ones, pair_in, pair_new, held, pair_r, pair_w, done_r, done_w,
):
    count, first = pair_in.shape[0], done_hbm.shape[0]

    def read(i):
        return pltpu.make_async_copy(
            pair_hbm.at[pl.ds(first + i * CHUNK, CHUNK)], pair_in.at[i], pair_r.at[i])

    def write(i):
        return pltpu.make_async_copy(
            pair_new.at[i], out_hbm.at[pl.ds(first + i * CHUNK, CHUNK)], pair_w.at[i])

    def fetch(i):
        return pltpu.make_async_copy(
            done_hbm.at[pl.ds(i * CHUNK, CHUNK)], held.at[i], done_r.at[i])

    def hand_on(i):
        return pltpu.make_async_copy(
            held.at[i], out_hbm.at[pl.ds(i * CHUNK, CHUNK)], done_w.at[i])

    for i in range(count):
        read(i).start()
    for i in range(first // CHUNK):
        fetch(i).start()
    pair_weights(w_in, half_in, ones)

    def step(i, carry):
        read(i).wait()

        def put_bias(t, b):
            bias_ref[pl.ds(pl.multiple_of(i * CHUNK * 16 + 16 * t, 16), 16), :] = b

        pair_new[i] = pair_chunk(pair_in[i], half_in, w_out, bias_t, g_pair, g_bias, ones, put_bias)
        write(i).start()
        for t in range(first // CHUNK):
            @pl.when(i == t * count // (first // CHUNK))
            def _():
                fetch(t).wait()
                hand_on(t).start()

        return carry

    lax.fori_loop(0, count, step, 0)
    for i in range(count):
        write(i).wait()
    for i in range(first // CHUNK):
        hand_on(i).wait()


def attend_kernel(
    q_ref, k_ref, v_ref, bias_early, bias_late, mask_ref, w_out, token_ref,
    out_ref,
    bias_ref,
    num_out, st_out, num_in, st_in, num_s, num_r, st_s, st_r,
):
    row, col = lax.axis_index("row"), lax.axis_index("col")
    barrier = pltpu.get_barrier_semaphore()
    for d in range(1, COLS):
        greet(barrier, row, (col + d) % COLS)

    split = bias_early.shape[0]
    bias_ref[:split] = bias_early[...]
    bias_ref[split:] = bias_late[...]
    head = lax.broadcasted_iota(jnp.int32, (16, 768), 0)
    lane = lax.broadcasted_iota(jnp.int32, (16, 768), 1)
    heads = jnp.where((lane >= head * HEAD) & (lane < head * HEAD + HEAD), 1.0, 0.0)
    eye = jnp.where(
        lax.broadcasted_iota(jnp.int32, (16, 128), 0) == lax.broadcasted_iota(jnp.int32, (16, 128), 1),
        1.0, 0.0,
    )
    masking = (mask_ref[...].astype(F32) - 1.0) * 1e9

    def chunk(c2):
        qs = q_ref[pl.ds(c2 * OWN, OWN), :].astype(F32)
        big = (qs[:, None, :] * heads[None]).reshape(256, 768).astype(BF16)
        s = dot_nt(big, k_ref[...]) * (HEAD ** -0.5)
        s = s + bias_ref[pl.ds(c2 * 256, 256), :] + masking
        top = jnp.max(s, axis=-1, keepdims=True)
        e = jnp.exp(s - top)
        total = jnp.sum(e, axis=-1, keepdims=True)
        o = dot(e.astype(BF16), v_ref[...])
        num = jnp.sum(o.reshape(OWN, 16, 768) * heads[None], axis=1)
        tops = jnp.sum(jnp.broadcast_to(top, (256, 128)).reshape(OWN, 16, 128) * eye[None], axis=1)
        totals = jnp.sum(jnp.broadcast_to(total, (256, 128)).reshape(OWN, 16, 128) * eye[None], axis=1)
        return num.astype(BF16), jnp.concatenate([tops, totals], axis=0)

    def send(d):
        c2 = (col + d) % COLS
        return (
            remote(num_out.at[c2], num_in.at[col], num_s.at[d], num_r.at[col], row, c2),
            remote(st_out.at[c2], st_in.at[col], st_s.at[d], st_r.at[col], row, c2),
        )

    def receive(d):
        c2 = (col + d) % COLS
        return (
            remote(num_out.at[c2], num_in.at[c2], num_s.at[d], num_r.at[c2], row, col),
            remote(st_out.at[c2], st_in.at[c2], st_s.at[d], st_r.at[c2], row, col),
        )

    for d in range(1, COLS):
        c2 = (col + d) % COLS
        num, st = chunk(c2)
        num_out[pl.ds(c2, 1)] = num[None]
        st_out[pl.ds(c2, 1)] = st[None]
        if d == 1:
            pl.semaphore_wait(barrier, COLS - 1)
        for copy in send(d):
            copy.start()
    num, st = chunk(col)
    num_in[pl.ds(col, 1)] = num[None]
    st_in[pl.ds(col, 1)] = st[None]
    for d in range(1, COLS):
        for copy in receive(d):
            copy.wait_recv()
    st = st_in[...]
    tops, totals = st[:, :OWN], st[:, OWN:]
    best = jnp.max(tops, axis=0, keepdims=True)
    w = jnp.exp(tops - best)
    den = jnp.sum(w * totals, axis=0)
    small = jnp.concatenate([w.reshape(COLS * OWN, 128), den], axis=0)
    wide = jnp.concatenate([heads, jnp.zeros((112, 768), F32)], axis=0)
    spread = jnp.dot(small, wide, preferred_element_type=F32, precision=lax.Precision.HIGHEST)
    num = jnp.zeros((OWN, 768), F32)
    for s in range(COLS):
        num = num + num_in[s].astype(F32) * spread[s * OWN:(s + 1) * OWN]
    mix = (num / spread[COLS * OWN:]).astype(BF16)
    out_ref[...] = (token_ref[...].astype(F32) + dot(mix, w_out[...])).astype(BF16)
    for d in range(1, COLS):
        for copy in send(d):
            copy.wait_send()


def body(
    atom_single, atom_to_token, token_mask, pair, w_atom_qkv, w_atom_out, w_aggregate,
    pair_gain, w_pair_in, w_pair_out, bias_gain, w_bias, token_gain, w_token_qkv, w_token_out,
):
    vmem = pl.BlockSpec(memory_space=pltpu.VMEM)
    anywhere = pl.BlockSpec(memory_space=pl.ANY)
    dma = pltpu.SemaphoreType.DMA
    nq, keys, chan = pair.shape
    early, late = EARLY, nq // CHUNK - EARLY
    g_pair, g_bias = pair_gain.reshape(1, chan), bias_gain.reshape(1, chan)
    prepared = [
        pltpu.VMEM((128, 512), BF16), pltpu.VMEM((128, 128), BF16),
    ]
    atom_out, token_in, q, k, v, done, bias_early = pl.pallas_call(
        tokens_kernel,
        in_specs=[anywhere] * 13,
        out_specs=[vmem] * 5 + [anywhere, vmem],
        out_shape=[
            jax.ShapeDtypeStruct((128, 128), BF16),
            jax.ShapeDtypeStruct((OWN, 768), BF16),
            jax.ShapeDtypeStruct((128, 768), BF16),
            jax.ShapeDtypeStruct((256, 768), BF16),
            jax.ShapeDtypeStruct((256, 768), BF16),
            jax.ShapeDtypeStruct((early * CHUNK, keys, chan), BF16),
            jax.ShapeDtypeStruct((early * CHUNK * 16, keys), F32),
        ],
        scratch_shapes=[
            pltpu.VMEM((128, 128), BF16), pltpu.VMEM((128, 128), jnp.int32),
            pltpu.VMEM((128, 384), BF16), pltpu.VMEM((128, 128), BF16),
            pltpu.VMEM((128, 768), BF16), pltpu.VMEM((6, 128), F32),
            pltpu.VMEM((768, 2304), BF16),
            pltpu.VMEM((128, 512), BF16), pltpu.VMEM((256, 128), BF16),
            pltpu.VMEM((16, 128), BF16), pltpu.VMEM((1, 128), F32), pltpu.VMEM((1, 128), F32),
            *prepared,
            pltpu.VMEM((early, CHUNK, keys, chan), BF16),
            pltpu.VMEM((early, CHUNK, keys, chan), BF16),
            pltpu.VMEM((224, 128), BF16),
            pltpu.VMEM((ROWS, 128, 128), BF16),
            pltpu.VMEM((COLS, OWN, 768), SUM_TYPE),
            pltpu.VMEM((COLS, OWN, 768), SUM_TYPE),
            pltpu.VMEM((OWN, 128), F32),
            pltpu.VMEM((OWN, 768), BF16),
            pltpu.VMEM((OWN, 768), BF16),
            pltpu.VMEM((OWN, 768), BF16),
            pltpu.VMEM((OWN, 768), BF16),
            pltpu.VMEM((COLS, OWN, 768), BF16),
            pltpu.VMEM((ROWS, OWN, 768), BF16),
            dma((12,)), dma((early,)), dma((early,)),
            dma((2,)), dma((2,)), dma((ROWS,)), dma((ROWS,)), dma((COLS,)), dma((COLS,)),
            dma((1,)), dma((1,)), dma((COLS,)), dma((COLS,)), dma((ROWS,)), dma((ROWS,)),
        ],
        compiler_params=pltpu.CompilerParams(
            collective_id=0, has_side_effects=True, vmem_limit_bytes=VMEM_LIMIT
        ),
        name="tokens",
    )(
        atom_single, atom_to_token.reshape(128, 128), w_atom_qkv, w_atom_out, w_aggregate,
        token_gain.reshape(6, 128), w_token_qkv,
        pair, w_pair_in, w_pair_out, w_bias.T, g_pair, g_bias,
    )
    pair_out, bias_late = pl.pallas_call(
        rest_kernel,
        in_specs=[anywhere, anywhere] + [vmem] * 5,
        out_specs=[anywhere, vmem],
        out_shape=[
            jax.ShapeDtypeStruct(pair.shape, BF16),
            jax.ShapeDtypeStruct((late * CHUNK * 16, keys), F32),
        ],
        scratch_shapes=[
            *prepared,
            pltpu.VMEM((late, CHUNK, keys, chan), BF16),
            pltpu.VMEM((late, CHUNK, keys, chan), BF16),
            pltpu.VMEM((early, CHUNK, keys, chan), BF16),
            dma((late,)), dma((late,)), dma((early,)), dma((early,)),
        ],
        compiler_params=pltpu.CompilerParams(vmem_limit_bytes=VMEM_LIMIT),
        name="pair",
    )(pair, done, w_pair_in, w_pair_out, w_bias.T, g_pair, g_bias)
    token_out = pl.pallas_call(
        attend_kernel,
        in_specs=[vmem] * 8,
        out_specs=vmem,
        out_shape=jax.ShapeDtypeStruct((OWN, 768), BF16),
        scratch_shapes=[
            pltpu.VMEM((nq * 16, keys), F32),
            pltpu.VMEM((COLS, OWN, 768), BF16),
            pltpu.VMEM((COLS, 2 * OWN, 128), F32),
            pltpu.VMEM((COLS, OWN, 768), BF16),
            pltpu.VMEM((COLS, 2 * OWN, 128), F32),
            dma((COLS,)), dma((COLS,)), dma((COLS,)), dma((COLS,)),
        ],
        compiler_params=pltpu.CompilerParams(
            collective_id=1, has_side_effects=True, vmem_limit_bytes=VMEM_LIMIT
        ),
        name="attend",
    )(q, k, v, bias_early, bias_late, token_mask.reshape(1, 256), w_token_out, token_in)
    return (atom_out, token_out, pair_out)


def solution(mesh):
    atoms = P(("row", "col"), None)
    pairs = P("row", "col", None)
    return jax.shard_map(
        body,
        mesh=mesh,
        in_specs=(atoms, P(), P("col"), pairs) + (P(),) * 11,
        out_specs=(atoms, atoms, pairs),
        check_vma=False,
    )
```

time: 103 us -> 75.8 us (0.74)
  Pallas kernels: 92.5 us -> 72.4 us
  local copies, waits for them, and re-layouts: 8.16 us -> 1.97 us
    pallas_call x3, Pallas kernels: 92.5 us -> 72.4 us  [the longest x1 47.7 us: body(): pl.pallas_call(tokens_kernel, in_specs=[anywhere] * 13, out_specs=[vmem]...]
    unnamed x26 -> x4, local copies, waits for them, and re-layouts: 7.42 us -> 1.97 us
where the time goes in v2:
time: 75.8 us; the launch traced here: 75.1 us
  Pallas kernels  72.4 us (96%)
  local copies, waits for them, and re-layouts  1.97 us (3%)
    pallas_call x1, Pallas kernels, body(): pl.pallas_call(tokens_kernel, in_specs=[anywhere] * 13, out_specs=[vmem]...  47.7 us
    pallas_call x1, Pallas kernels, body(): pl.pallas_call(attend_kernel, in_specs=[vmem] * 8, out_specs=vmem, out_sh...  13.9 us
    pallas_call x1, Pallas kernels, body(): pl.pallas_call(rest_kernel, in_specs=[anywhere, anywhere] + [vmem] * 5, o...  10.8 us
    unnamed x4, local copies, waits for them, and re-layouts  1.97 us

profile of v2, /device:TPU:0, one launch (start us, length us, event | category | flops | bytes accessed | tf_op | source)
XLA Modules:
  0.0 75.1 jit_solution(17099612699251387033)
XLA Ops:
  0.6 47.7 %tokens.1 = (bf16[128,128]{1,0:T(8,128)(2,1)}, bf16[16,768]{1,0:T(8,128)(2,1)}, bf16[128,768]{1,0:T(8,128)(2,1)}, bf16[256,768]{1,0:T(8,128)(2,1)}, bf16[256,768...) custom-call(bf16[128,128]{1,0:T(8,128)(2,1)} %atom_hbm.1, s32[128,128]{1,0:T(8,128)} %bitcast.6, ...), custom_call_target="tpu_custom_call" | custom-call | tf_op jit(solution)/shard_map/tokens/pallas_call | solution.py:459
  48.3 0.0 copy-start
  48.3 10.8 %pair.1 = (bf16[128,256,128]{2,1,0:T(8,128)(2,1)}, f32[256,256]{1,0:T(8,128)}) custom-call(bf16[128,256,128]{2,1,0:T(8,128)(2,1)} %pair_hbm.3, bf16[112,256,128]{2,1,0:T(8,128)(2,1)} %get-tuple-element.17.done_hbm, bf16[128,512]{1,0:T(8,128)(2,1)} %w_in.1, bf16[256,128]{1,0:T(8,128)(2,1)} %w_out.2, bf16[16,128]{1,0:T(8,128)(2,1)} %bitcast.8, ...), custom_call_target="tpu_custom_call" | custom-call | tf_op jit(solution)/shard_map/pair/pallas_call | solution.py:506
  59.2 13.9 %attend.1 = bf16[16,768]{1,0:T(8,128)(2,1)} custom-call(bf16[128,768]{1,0:T(8,128)(2,1)} %get-tuple-element.13.q_ref, bf16[256,768]{1,0:T(8,128)(2,1)} %get-tuple-element.14.k_ref, bf16[256,768]{1,0:T(8,128)(2,1)} %get-tuple-element.15.v_ref, f32[1792,256]{1,0:T(8,128)} %get-tuple-element.16.bias_early, f32[256,256]{1,0:T(8,128)} %get-tuple-element.18.bias_late, ...), custom_call_target="tpu_custom_call" | custom-call | tf_op jit(solution)/shard_map/attend/pallas_call | solution.py:524
  73.1 0.0 copy-done
  73.1 0.6 copy.20
  73.7 1.3 %copy.21 = bf16[16,768]{1,0:T(8,128)(2,1)} copy(bf16[16,768]{1,0:T(8,128)(2,1)} %attend.1) | data formatting | bytes 49152
Async XLA Ops:
  48.3 24.8 %copy-start = (bf16[128,128]{1,0:T(8,128)(2,1)S(1)}, bf16[128,128]{1,0:T(8,128)(2,1)}, u32[]{:S(2)}) copy-start(bf16[128,128]{1,0:T(8,128)(2,1)} %get-tuple-element.24) | copy-start | bytes 98308

commit v3 on v2

v3 whole, which is shorter than its diff:
```python
import functools

import jax
import jax.numpy as jnp
from jax import lax
from jax.experimental import pallas as pl
from jax.experimental.pallas import tpu as pltpu
from jax.sharding import PartitionSpec as P

F32, BF16 = jnp.float32, jnp.bfloat16
MESH = pl.DeviceIdType.MESH
NT = (((1,), (1,)), ((), ()))
ROWS, COLS = 16, 8
WINDOW, KEYS, HALO = 32, 128, 48
ATOM_HEADS, TOKEN_HEADS, HEAD = 4, 16, 48
OWN = 16
VMEM_LIMIT = 56 << 20
SUM_TYPE = BF16
CHUNK = 16
BEFORE = 6
GROUPS = (6,)
STAGES = (0, 1, 3, 4)


def dot(a, b):
    return jnp.dot(a, b, preferred_element_type=F32)


def dot_nt(a, b):
    return lax.dot_general(a, b, NT, preferred_element_type=F32)


def remote(src, dst, send, recv, row, col):
    return pltpu.make_async_remote_copy(
        src_ref=src, dst_ref=dst, send_sem=send, recv_sem=recv,
        device_id=(row, col), device_id_type=MESH,
    )


def greet(sem, row, col):
    pl.semaphore_signal(sem, inc=1, device_id=(row, col), device_id_type=MESH)


def atom_attention(x, me, atoms_total, w_qkv, w_out):
    n = 128
    qkv = dot(x, w_qkv).astype(BF16)
    q = qkv[HALO:HALO + n, :128]
    k, v = qkv[:, 128:256], qkv[:, 256:]
    pad = jnp.zeros((256 - k.shape[0], 128), BF16)
    k = jnp.concatenate([k, pad], axis=0)
    v = jnp.concatenate([v, pad], axis=0)
    lane = lax.broadcasted_iota(jnp.int32, (n, 128), 1)
    parts = []
    for h in range(ATOM_HEADS):
        keep = (lane >= 32 * h) & (lane < 32 * h + 32)
        parts.append(jnp.where(keep, q.astype(F32), 0.0).astype(BF16))
    s = dot_nt(jnp.concatenate(parts, axis=0), k) * (32.0 ** -0.5)
    atom = lax.broadcasted_iota(jnp.int32, (n, 256), 0)
    key = lax.broadcasted_iota(jnp.int32, (n, 256), 1)
    first = (atom // WINDOW) * WINDOW
    place = key - HALO + me * n
    shift = jnp.where((place >= 0) & (place < atoms_total), 0.0, -1e9)
    inside = (key >= first) & (key < first + KEYS)
    out = jnp.zeros((n, 128), F32)
    for h in range(ATOM_HEADS):
        sh = jnp.where(inside, s[h * n:(h + 1) * n] + shift, -1e30)
        e = jnp.exp(sh - jnp.max(sh, axis=-1, keepdims=True))
        total = jnp.sum(e, axis=-1, keepdims=True)
        o = dot(e.astype(BF16), v) / total
        keep = (lane >= 32 * h) & (lane < 32 * h + 32)
        out = jnp.where(keep, o, out)
    own = x[HALO:HALO + n].astype(F32)
    return (own + dot(out.astype(BF16), w_out)).astype(BF16)


def norm_rows(x_bf, gain, ones):
    x = x_bf.astype(F32)
    xc = x - dot(x_bf, ones)
    var = jnp.mean(xc * xc, axis=-1, keepdims=True)
    return x, (xc * lax.rsqrt(var + 1e-5) * gain).astype(BF16)


def pair_weights(w_in, half_in, ones):
    half_in[:, :256] = w_in[:, :256] * jnp.asarray(0.5, BF16)
    half_in[:, 256:] = w_in[:, 256:]
    ones[...] = jnp.full(ones.shape, 1.0 / 128.0, BF16)


def pair_chunk(x, w_in, w_out, bias_t, g_pair, g_bias, ones, put_bias):
    n, keys, chan = x.shape
    x, normed = norm_rows(x.reshape(n * keys, chan), g_pair[...], ones[...])
    both = dot(normed, w_in[...])
    half, up = both[:, :256], both[:, 256:]
    hidden = ((half + half * jnp.tanh(half)) * up).astype(BF16)
    new = (x + dot(hidden, w_out[...])).astype(BF16)
    _, normed = norm_rows(new, g_bias[...], ones[...])
    for t in range(n):
        put_bias(t, dot_nt(bias_t[...], normed[t * keys:(t + 1) * keys]))
    return new.reshape(n, keys, chan)


def token_norm(t, gain):
    gain = jnp.concatenate([gain[i:i + 1] for i in range(6)], axis=1)
    t = t.astype(F32)
    tc = t - jnp.mean(t, axis=-1, keepdims=True)
    var = jnp.mean(tc * tc, axis=-1, keepdims=True)
    return (tc * lax.rsqrt(var + 1e-5) * gain).astype(BF16)


def step_kernel(
    atom_hbm, ids_hbm, w_aqkv_hbm, w_aout_hbm, w_agg_hbm, gain_hbm, w_qkv_hbm, mask_hbm,
    pair_hbm, w_in_hbm, w_out_hbm, bias_t_hbm, g_pair_hbm, g_bias_hbm,
    atom_out_hbm, token_hbm, num_hbm, pair_out_hbm,
    atom, ids, w_aqkv, w_aout, w_agg, gain, w_qkv, mask, w_in, w_out, bias_t, g_pair, g_bias,
    half_in, ones, pair_in, pair_new, bias,
    x_buf, gathered, sums, parts, counts, key_token, hot, tq, tk,
    query, key, value, num_out, num_in, atom_out,
    load, store, pair_r, pair_w,
    halo_s, halo_r, gat_s, gat_r, sum_s, sum_r, tq_s, tq_r, tk_s, tk_r,
    num_s, num_r,
):
    row, col = lax.axis_index("row"), lax.axis_index("col")
    me = row * COLS + col
    left, right = (me + 127) % 128, (me + 1) % 128
    twin = row + 1 - 2 * (row % 2)
    q_row, q_col = 2 * col + row // COLS, row // 2
    stays = (q_row == row).astype(jnp.int32)

    pairs = [
        (w_in_hbm, w_in), (w_out_hbm, w_out), (bias_t_hbm, bias_t), (g_pair_hbm, g_pair),
        (g_bias_hbm, g_bias), (atom_hbm, atom), (ids_hbm, ids), (w_aqkv_hbm, w_aqkv),
        (w_aout_hbm, w_aout), (w_agg_hbm, w_agg), (gain_hbm, gain), (w_qkv_hbm, w_qkv),
        (mask_hbm, mask),
    ]
    loads = [pltpu.make_async_copy(a, b, load.at[i]) for i, (a, b) in enumerate(pairs)]
    chunks = pair_in.shape[0]

    def owner(i):
        return (col + 1 + i) % COLS

    def rows_of(i):
        return pl.ds(pl.multiple_of(owner(i) * CHUNK, CHUNK), CHUNK)

    def read(i):
        return pltpu.make_async_copy(pair_hbm.at[rows_of(i)], pair_in.at[i], pair_r.at[i])

    def write(i):
        return pltpu.make_async_copy(pair_new.at[i], pair_out_hbm.at[pl.ds(i * CHUNK, CHUNK)], pair_w.at[i])

    loads[5].start()
    for copy in loads[:5]:
        copy.start()
    read(0).start()
    for copy in loads[6:]:
        copy.start()
    for i in range(1, chunks):
        read(i).start()

    barrier = pltpu.get_barrier_semaphore()
    greet(barrier, left // COLS, left % COLS)
    greet(barrier, right // COLS, right % COLS)
    greet(barrier, twin, col)
    for d in range(2, ROWS, 2):
        greet(barrier, (row + d) % ROWS, col)
    for d in range(1, COLS):
        greet(barrier, row, (col + d) % COLS)

    for i in range(COLS):
        @pl.when((stays == 0) | (row % COLS != i))
        def _():
            greet(barrier, COLS * (row % 2) + i, q_col)

    to_right = remote(atom.at[pl.ds(80, 48)], x_buf.at[pl.ds(0, 48)],
                      halo_s.at[0], halo_r.at[0], right // COLS, right % COLS)
    to_left = remote(atom.at[pl.ds(0, 48)], x_buf.at[pl.ds(176, 48)],
                     halo_s.at[1], halo_r.at[1], left // COLS, left % COLS)

    core, chip = row % 2, row // 2

    def spread(buf, send, recv, d):
        block = buf.at[core, chip]
        return remote(block, block, send.at[d], recv.at[chip], (row + 2 * d) % ROWS, col)

    def arrival(buf, send, recv, j):
        block = buf.at[core, j]
        return remote(block, block, send.at[0], recv.at[j], row, col)

    def hand_over(buf, send, recv, half, c):
        blocks = buf.at[c, pl.ds(4 * half, 4)]
        return remote(blocks, blocks, send.at[8 + half], recv.at[8 + half], twin, col)

    def start_spread(buf, send, recv):
        for d in range(1, 8):
            spread(buf, send, recv, d).start()

    def pass_on(buf, send, recv, half):
        for j in range(4 * half, 4 * half + 4):
            @pl.when(chip != j)
            def _():
                arrival(buf, send, recv, j).wait_recv()

        hand_over(buf, send, recv, half, core).start()

    def handed(buf, send, recv, half):
        hand_over(buf, send, recv, half, 1 - core).wait_recv()

    def drain_spread(buf, send, recv):
        for d in range(1, 8):
            spread(buf, send, recv, d).wait_send()
        for half in range(2):
            hand_over(buf, send, recv, half, core).wait_send()

    atoms_move = (gathered, gat_s, gat_r)
    keys_move = (tk, tk_s, tk_r)

    def send_sum(d):
        c2 = (col + d) % COLS
        return remote(sums.at[c2], parts.at[col], sum_s.at[d], sum_r.at[col], row, c2)

    def recv_sum(d):
        c2 = (col + d) % COLS
        return remote(sums.at[c2], parts.at[c2], sum_s.at[d], sum_r.at[c2], row, col)

    def send_q(d):
        return remote(key_token, tq.at[row % COLS], tq_s.at[d], tq_r.at[row % COLS], q_row, (col + d) % COLS)

    def recv_q(i):
        return remote(key_token, tq.at[i], tq_s.at[i], tq_r.at[i], row, col)

    def start_gather():
        for copy in loads[6:]:
            copy.wait()
        to_right.wait()
        to_left.wait()
        atom_out[...] = atom_attention(x_buf[...], me, 128 * 128, w_aqkv[...], w_aout[...])
        gathered[pl.ds(core, 1), pl.ds(chip, 1)] = atom_out[...][None, None]
        start_spread(*atoms_move)
        own_tokens = col * 256 + row * OWN + lax.broadcasted_iota(jnp.int32, (OWN, 128), 0)
        acc = jnp.zeros((OWN, 128), F32)
        for t in range(128):
            acc = acc + (own_tokens == ids[t:t + 1, :]).astype(F32)
        counts[...] = jnp.broadcast_to(jnp.sum(acc, axis=-1, keepdims=True), (OWN, 128))

        place = lax.broadcasted_iota(jnp.int32, (128, 128), 0)
        token = (place // OWN) * 256 + row * OWN + place % OWN
        for c in range(2):
            for j in range(8):
                here = ids[pl.ds(COLS * (2 * j + c) + col, 1), :]
                hot[c, :, 128 * j:128 * j + 128] = (token == here).astype(F32).astype(BF16)

    def part_sums(c, half):
        x = gathered[c, 4 * half:4 * half + 4].reshape(512, 128)
        proj = jnp.maximum(dot(x, w_agg[...]), 0.0).astype(BF16)
        return dot(hot[c, :, 512 * half:512 * half + 512], proj)

    def start_sums():
        pass_on(*atoms_move, 0)
        pass_on(*atoms_move, 1)
        total = part_sums(core, 0) + part_sums(core, 1)
        handed(*atoms_move, 0)
        total = total + part_sums(1 - core, 0)
        handed(*atoms_move, 1)
        total = total + part_sums(1 - core, 1)
        sums[...] = total.astype(sums.dtype).reshape(COLS, OWN, 768)
        for d in range(1, COLS):
            send_sum(d).start()
        parts[pl.ds(col, 1)] = sums[pl.ds(col, 1)]

    def start_keys():
        for d in range(1, COLS):
            recv_sum(d).wait_recv()
        acc = parts[0].astype(F32)
        for s in range(1, COLS):
            acc = acc + parts[s].astype(F32)
        token_in = (acc / counts[:, :1]).astype(BF16)
        key_token[...] = token_in
        tk[pl.ds(core, 1), pl.ds(chip, 1)] = token_norm(token_in, gain[...])[None, None]
        start_spread(*keys_move)
        for d in range(1, COLS):
            send_q(d).start()

        @pl.when(stays == 0)
        def _():
            send_q(0).start()

        @pl.when(stays == 1)
        def _():
            tq[pl.ds(row % COLS, 1)] = token_in[None]

    def pass_keys():
        pass_on(*keys_move, 0)
        pass_on(*keys_move, 1)

    stages = (start_gather, start_sums, start_keys, pass_keys)

    def pair_step(i):
        read(i).wait()

        def put_bias(t, b):
            bias[pl.ds(pl.multiple_of(i * CHUNK * 16 + 16 * t, 16), 16), :] = b

        pair_new[i] = pair_chunk(pair_in[i], half_in, w_out, bias_t, g_pair, g_bias, ones, put_bias)
        write(i).start()

    def step(i, carry):
        pair_step(i)
        for at, stage in zip(STAGES, stages):
            pl.when(i == at)(stage)
        return carry

    loads[5].wait()
    x_buf[HALO:HALO + 128] = atom[...]
    pl.semaphore_wait(barrier, 2 + 1 + 7 + 7 + 8 - stays)
    to_right.start()
    to_left.start()
    for copy in loads[:5]:
        copy.wait()
    pair_weights(w_in, half_in, ones)
    lax.fori_loop(0, BEFORE, step, 0)

    for i in range(COLS):
        @pl.when((stays == 0) | (row % COLS != i))
        def _():
            recv_q(i).wait_recv()

    for i in range(COLS):
        query[i * OWN:(i + 1) * OWN, :] = token_norm(tq[pl.ds(owner(i), 1)].reshape(OWN, 768), gain[...])
    query[...] = dot(query[...], w_qkv[:, :768]).astype(BF16)
    handed(*keys_move, 0)
    handed(*keys_move, 1)
    tkv = jnp.concatenate([tk[j % 2, j // 2] for j in range(ROWS)], axis=0)
    key[...] = dot(tkv, w_qkv[:, 768:1536]).astype(BF16)
    value[...] = dot(tkv, w_qkv[:, 1536:]).astype(BF16)

    results = [
        (atom_out, atom_out_hbm), (tq.at[col], token_hbm), (num_in, num_hbm),
    ]
    stores = [pltpu.make_async_copy(a, b, store.at[i]) for i, (a, b) in enumerate(results)]
    for copy in stores[:2]:
        copy.start()

    def send(i):
        return remote(num_out.at[i], num_in.at[col], num_s.at[i], num_r.at[col], row, owner(i))

    def receive(i):
        c2 = owner(i)
        return remote(num_out.at[i], num_in.at[c2], num_s.at[i], num_r.at[c2], row, col)

    def attend_slots(first, count):
        return attend(query[first * OWN:(first + count) * OWN, :],
                      bias[first * 256:(first + count) * 256, :], key, value, mask)

    def send_slots(first, count):
        num_out[first:first + count] = attend_slots(first, count)
        for i in range(first, first + count):
            send(i).start()

    first = 0
    for count in GROUPS:
        send_slots(first, count)
        first += count
    for i in range(first, chunks - 1):
        pair_step(i)
        send_slots(i, 1)
    if BEFORE < chunks:
        pair_step(chunks - 1)
    num_in[pl.ds(col, 1)] = attend_slots(chunks - 1, 1)

    drain_spread(*atoms_move)
    drain_spread(*keys_move)
    for d in range(1, COLS):
        send_sum(d).wait_send()
        send_q(d).wait_send()

    @pl.when(stays == 0)
    def _():
        send_q(0).wait_send()

    for i in range(chunks):
        write(i).wait()
    for i in range(COLS - 1):
        send(i).wait_send()
    for i in range(COLS - 1):
        receive(i).wait_recv()
    for copy in stores[2:]:
        copy.start()
    for copy in stores:
        copy.wait()


def head_lanes():
    head = lax.broadcasted_iota(jnp.int32, (16, 768), 0)
    lane = lax.broadcasted_iota(jnp.int32, (16, 768), 1)
    return jnp.where((lane >= head * HEAD) & (lane < head * HEAD + HEAD), 1.0, 0.0)


def pack_heads(column, n):
    lane = lax.broadcasted_iota(jnp.int32, (16, 128), 1)
    head = lax.broadcasted_iota(jnp.int32, (16, 128), 0)
    mine = jnp.where(lane % 16 == head, 1.0, 0.0)
    wide = jnp.sum(jnp.broadcast_to(column, (n * 16, 128)).reshape(n, 16, 128) * mine[None], axis=1)
    return jnp.sum(wide.reshape(n // 8, 8, 128) * token_lanes()[None], axis=1)


def token_lanes():
    lane = lax.broadcasted_iota(jnp.int32, (8, 128), 1)
    return jnp.where(lane // 16 == lax.broadcasted_iota(jnp.int32, (8, 128), 0), 1.0, 0.0)


def attend(query, bias, key, value, mask):
    n = query.shape[0]
    heads = head_lanes()
    masking = (mask[...].astype(F32) - 1.0) * 1e9
    big = (query.astype(F32)[:, None, :] * heads[None]).reshape(n * 16, 768).astype(BF16)
    s = dot_nt(big, key[...]) * (HEAD ** -0.5)
    s = s + bias + masking
    top = jnp.max(s, axis=-1, keepdims=True)
    e = jnp.exp(s - top)
    total = jnp.sum(e, axis=-1, keepdims=True)
    o = dot(e.astype(BF16), value[...])
    num = jnp.sum(o.reshape(n, 16, 768) * heads[None], axis=1).astype(BF16)
    tops, totals = pack_heads(top, n), pack_heads(total, n)
    parts = split_rows(tops, 3) + split_rows(totals, 2)
    rest = jnp.zeros((6, 128), F32)
    st = [
        jnp.concatenate([p[2 * i:2 * i + 2] for p in parts] + [rest], axis=0)
        for i in range(n // OWN)
    ]
    st = jnp.concatenate(st, axis=0).astype(BF16)
    return jnp.concatenate([num, st], axis=1).reshape(n // OWN, OWN, 896)


def split_rows(x, count):
    parts = []
    for _ in range(count):
        part = x.astype(BF16).astype(F32)
        parts.append(part)
        x = x - part
    return parts


def finish_kernel(
    done_hbm, atom_hbm, token_hbm, num_hbm, w_tout_hbm,
    pair_out_hbm, atom_out_hbm, token_out_hbm,
    atom, token, num_in, w_tout, held, token_out,
    load, done_r, done_w, store,
):
    col = lax.axis_index("col")
    count = held.shape[0]
    pairs = [(num_hbm, num_in), (w_tout_hbm, w_tout), (token_hbm, token), (atom_hbm, atom)]
    loads = [pltpu.make_async_copy(a, b, load.at[i]) for i, (a, b) in enumerate(pairs)]

    def rows_of(i):
        return pl.ds(pl.multiple_of((col + 1 + i) % COLS * CHUNK, CHUNK), CHUNK)

    def fetch(i):
        return pltpu.make_async_copy(done_hbm.at[pl.ds(i * CHUNK, CHUNK)], held.at[i], done_r.at[i])

    def hand_on(i):
        return pltpu.make_async_copy(held.at[i], pair_out_hbm.at[rows_of(i)], done_w.at[i])

    stores = [
        pltpu.make_async_copy(atom, atom_out_hbm, store.at[0]),
        pltpu.make_async_copy(token_out, token_out_hbm, store.at[1]),
    ]
    for i in range(count):
        fetch(i).start()
        if i == 1:
            for copy in loads:
                copy.start()
    for i in range(count):
        fetch(i).wait()
        hand_on(i).start()
    for copy in loads:
        copy.wait()
    stores[0].start()
    st = num_in[:, :, 768:].astype(F32)
    tops = st[:, 0:2] + st[:, 2:4] + st[:, 4:6]
    totals = st[:, 6:8] + st[:, 8:10]
    w = jnp.exp(tops - jnp.max(tops, axis=0, keepdims=True))
    den = jnp.sum(w * totals, axis=0)
    lanes = token_lanes()
    small = [
        jnp.broadcast_to(part[t:t + 1], (8, 128)) * lanes
        for part in [w[s] for s in range(COLS)] + [den] for t in range(2)
    ]
    wide = jnp.concatenate([head_lanes()] * 8, axis=0)
    spread = jnp.dot(jnp.concatenate(small, axis=0), wide, preferred_element_type=F32,
                     precision=lax.Precision.HIGHEST)
    acc = jnp.zeros((OWN, 768), F32)
    for s in range(COLS):
        acc = acc + num_in[s, :, :768].astype(F32) * spread[s * OWN:(s + 1) * OWN]
    mix = (acc / spread[COLS * OWN:]).astype(BF16)
    token_out[...] = (token[...].astype(F32) + dot(mix, w_tout[...])).astype(BF16)
    stores[1].start()
    for i in range(count):
        hand_on(i).wait()
    for copy in stores:
        copy.wait()


def body(
    atom_single, atom_to_token, token_mask, pair, w_atom_qkv, w_atom_out, w_aggregate,
    pair_gain, w_pair_in, w_pair_out, bias_gain, w_bias, token_gain, w_token_qkv, w_token_out,
):
    vmem = pl.BlockSpec(memory_space=pltpu.VMEM)
    anywhere = pl.BlockSpec(memory_space=pl.ANY)
    dma = pltpu.SemaphoreType.DMA
    nq, keys, chan = pair.shape
    chunks = nq // CHUNK
    block = pltpu.VMEM((OWN, 768), BF16)
    columns = pltpu.VMEM((COLS, OWN, 768), BF16)
    mixed = pltpu.VMEM((COLS, OWN, 896), BF16)
    taken = (CHUNK, keys, chan)
    pair_args = [
        pltpu.VMEM((128, 512), BF16), pltpu.VMEM((256, 128), BF16), pltpu.VMEM((16, 128), BF16),
        pltpu.VMEM((1, 128), F32), pltpu.VMEM((1, 128), F32),
    ]
    prepared = [pltpu.VMEM((128, 512), BF16), pltpu.VMEM((128, 128), BF16)]
    keyed = pltpu.VMEM((256, 768), BF16)
    pair_weights_in = (
        w_pair_in, w_pair_out, w_bias.T, pair_gain.reshape(1, chan), bias_gain.reshape(1, chan),
    )
    mask = token_mask.reshape(1, keys)
    atom_out, token_in, num, done = pl.pallas_call(
        step_kernel,
        in_specs=[anywhere] * 14,
        out_specs=[anywhere] * 4,
        out_shape=[
            jax.ShapeDtypeStruct((128, 128), BF16),
            jax.ShapeDtypeStruct((OWN, 768), BF16),
            jax.ShapeDtypeStruct((COLS, OWN, 896), BF16),
            jax.ShapeDtypeStruct(pair.shape, BF16),
        ],
        scratch_shapes=[
            pltpu.VMEM((128, 128), BF16), pltpu.VMEM((128, 128), jnp.int32),
            pltpu.VMEM((128, 384), BF16), pltpu.VMEM((128, 128), BF16),
            pltpu.VMEM((128, 768), BF16), pltpu.VMEM((6, 128), F32),
            pltpu.VMEM((768, 2304), BF16), pltpu.VMEM((1, 256), jnp.int32),
            *pair_args, *prepared,
            pltpu.VMEM((chunks, *taken), BF16),
            pltpu.VMEM((chunks, *taken), BF16),
            pltpu.VMEM((nq * 16, keys), F32),
            pltpu.VMEM((224, 128), BF16),
            pltpu.VMEM((2, 8, 128, 128), BF16),
            pltpu.VMEM((COLS, OWN, 768), SUM_TYPE),
            pltpu.VMEM((COLS, OWN, 768), SUM_TYPE),
            pltpu.VMEM((OWN, 128), F32),
            block, pltpu.VMEM((2, 128, 1024), BF16),
            columns,
            pltpu.VMEM((2, 8, OWN, 768), BF16),
            pltpu.VMEM((128, 768), BF16), keyed, keyed,
            mixed, mixed, pltpu.VMEM((128, 128), BF16),
            dma((13,)), dma((3,)), dma((chunks,)), dma((chunks,)),
            dma((2,)), dma((2,)), dma((16,)), dma((16,)), dma((COLS,)), dma((COLS,)),
            dma((COLS,)), dma((COLS,)), dma((16,)), dma((16,)),
            dma((COLS,)), dma((COLS,)),
        ],
        compiler_params=pltpu.CompilerParams(
            collective_id=0, has_side_effects=True, vmem_limit_bytes=VMEM_LIMIT
        ),
        name="step",
    )(
        atom_single, atom_to_token.reshape(128, 128), w_atom_qkv, w_atom_out, w_aggregate,
        token_gain.reshape(6, 128), w_token_qkv, mask, pair, *pair_weights_in,
    )
    pair_out, atom_out, token_out = pl.pallas_call(
        finish_kernel,
        in_specs=[anywhere] * 5,
        out_specs=[anywhere] * 3,
        out_shape=[
            jax.ShapeDtypeStruct(pair.shape, BF16),
            jax.ShapeDtypeStruct((128, 128), BF16),
            jax.ShapeDtypeStruct((OWN, 768), BF16),
        ],
        scratch_shapes=[
            pltpu.VMEM((128, 128), BF16), block, mixed, pltpu.VMEM((768, 768), BF16),
            pltpu.VMEM((chunks, *taken), BF16), block,
            dma((4,)), dma((chunks,)), dma((chunks,)), dma((2,)),
        ],
        compiler_params=pltpu.CompilerParams(vmem_limit_bytes=VMEM_LIMIT),
        name="finish",
    )(done, atom_out, token_in, num, w_token_out)
    return (atom_out, token_out, pair_out)


def solution(mesh):
    atoms = P(("row", "col"), None)
    pairs = P("row", "col", None)
    return jax.shard_map(
        body,
        mesh=mesh,
        in_specs=(atoms, P(), P("col"), pairs) + (P(),) * 11,
        out_specs=(atoms, atoms, pairs),
        check_vma=False,
    )
```

time: 75.8 us -> 59.1 us (0.78)
  Pallas kernels: 72.4 us -> 57.3 us
  local copies, waits for them, and re-layouts: 1.97 us -> 0 us
    pallas_call x3 -> x2, Pallas kernels: 72.4 us -> 57.3 us  [the longest x1 49.8 us: body(): pl.pallas_call(step_kernel, in_specs=[anywhere] * 14, out_specs=[anywhere...]
    unnamed x4 -> x0, local copies, waits for them, and re-layouts: 1.97 us -> none
where the time goes in v3:
time: 59.1 us; the launch traced here: 58.1 us
  Pallas kernels  57.3 us (97%)
  between operations  0.8 us (1%)
    pallas_call x1, Pallas kernels, body(): pl.pallas_call(step_kernel, in_specs=[anywhere] * 14, out_specs=[anywhere...  49.8 us
    pallas_call x1, Pallas kernels, body(): pl.pallas_call(finish_kernel, in_specs=[anywhere] * 5, out_specs=[anywher...  7.47 us

profile of v3, /device:TPU:0, one launch (start us, length us, event | category | flops | bytes accessed | tf_op | source)
XLA Modules:
  0.0 58.1 jit_solution(5978006851026994787)
XLA Ops:
  0.6 49.8 %step.1 = (bf16[128,128]{1,0:T(8,128)(2,1)}, bf16[16,768]{1,0:T(8,128)(2,1)}, bf16[8,16,896]{2,1,0:T(8,128)(2,1)}, bf16[128,256,128]{2,1,0:T(8,128)(2,1)}) custom-call(bf16[128,128]{1,0:T(8,128)(2,1)} %atom_hbm.1, s32[128,128]{1,0:T(8,128)} %bitcast.6, bf16[128,384]{1,0:T(8,128)(2,1)} %w_aqkv_hbm.1, bf16[128,128]{1,0:T(8,128)(2,1)} %w_aout_hbm.1, ...), custom_call_target="tpu_custom_call" | custom-call | tf_op jit(solution)/shard_map/step/pallas_call | solution.py:525
  50.5 7.5 %finish.1 = (bf16[128,256,128]{2,1,0:T(8,128)(2,1)}, bf16[128,128]{1,0:T(8,128)(2,1)}, bf16[16,768]{1,0:T(8,128)(2,1)}) custom-call(bf16[128,256,128]{2,1,0:T(8,128)(2,1)} %get-tuple-element.10.done_hbm, bf16[128,128]{1,0:T(8,128)(2,1)} %get-tuple-element.11.atom_hbm, bf16[16,768]{1,0:T(8,128)(2,1)} %get-tuple-element.12.token_hbm, ...), custom_call_target="tpu_custom_call" | custom-call | tf_op jit(solution)/shard_map/finish/pallas_call | solution.py:567

commit v4 on v3

--- a/solution.py
+++ b/solution.py
@@ -14,12 +14,12 @@
 WINDOW, KEYS, HALO = 32, 128, 48
 ATOM_HEADS, TOKEN_HEADS, HEAD = 4, 16, 48
 OWN = 16
-VMEM_LIMIT = 56 << 20
+VMEM_LIMIT = 48 << 20
 SUM_TYPE = BF16
 CHUNK = 16
-BEFORE = 6
-GROUPS = (6,)
-STAGES = (0, 1, 3, 4)
+BEFORE = 7
+GROUPS = (4, 3)
+STAGES = (0, 1, 3, 5)
 
 
 def dot(a, b):
@@ -110,12 +110,12 @@
 def step_kernel(
     atom_hbm, ids_hbm, w_aqkv_hbm, w_aout_hbm, w_agg_hbm, gain_hbm, w_qkv_hbm, mask_hbm,
     pair_hbm, w_in_hbm, w_out_hbm, bias_t_hbm, g_pair_hbm, g_bias_hbm,
-    atom_out_hbm, token_hbm, num_hbm, pair_out_hbm,
+    atom_out, token_out, num_final, pair_new,
     atom, ids, w_aqkv, w_aout, w_agg, gain, w_qkv, mask, w_in, w_out, bias_t, g_pair, g_bias,
-    half_in, ones, pair_in, pair_new, bias,
+    half_in, ones, pair_in, bias,
     x_buf, gathered, sums, parts, counts, key_token, hot, tq, tk,
-    query, key, value, num_out, num_in, atom_out,
-    load, store, pair_r, pair_w,
+    query, key, value, num_out, num_in,
+    load, pair_r,
     halo_s, halo_r, gat_s, gat_r, sum_s, sum_r, tq_s, tq_r, tk_s, tk_r,
     num_s, num_r,
 ):
@@ -143,9 +143,6 @@
 
     def read(i):
         return pltpu.make_async_copy(pair_hbm.at[rows_of(i)], pair_in.at[i], pair_r.at[i])
-
-    def write(i):
-        return pltpu.make_async_copy(pair_new.at[i], pair_out_hbm.at[pl.ds(i * CHUNK, CHUNK)], pair_w.at[i])
 
     loads[5].start()
     for copy in loads[:5]:
@@ -300,7 +297,6 @@
             bias[pl.ds(pl.multiple_of(i * CHUNK * 16 + 16 * t, 16), 16), :] = b
 
         pair_new[i] = pair_chunk(pair_in[i], half_in, w_out, bias_t, g_pair, g_bias, ones, put_bias)
-        write(i).start()
 
     def step(i, carry):
         pair_step(i)
@@ -332,12 +328,7 @@
     key[...] = dot(tkv, w_qkv[:, 768:1536]).astype(BF16)
     value[...] = dot(tkv, w_qkv[:, 1536:]).astype(BF16)
 
-    results = [
-        (atom_out, atom_out_hbm), (tq.at[col], token_hbm), (num_in, num_hbm),
-    ]
-    stores = [pltpu.make_async_copy(a, b, store.at[i]) for i, (a, b) in enumerate(results)]
-    for copy in stores[:2]:
-        copy.start()
+    token_out[...] = tq[pl.ds(col, 1)].reshape(OWN, 768)
 
     def send(i):
         return remote(num_out.at[i], num_in.at[col], num_s.at[i], num_r.at[col], row, owner(i))
@@ -376,16 +367,11 @@
     def _():
         send_q(0).wait_send()
 
-    for i in range(chunks):
-        write(i).wait()
     for i in range(COLS - 1):
         send(i).wait_send()
     for i in range(COLS - 1):
         receive(i).wait_recv()
-    for copy in stores[2:]:
-        copy.start()
-    for copy in stores:
-        copy.wait()
+    num_final[...] = num_in[...]
 
 
 def head_lanes():
@@ -440,21 +426,17 @@
 
 
 def finish_kernel(
-    done_hbm, atom_hbm, token_hbm, num_hbm, w_tout_hbm,
+    held, atom, token, num_in, w_tout_hbm,
     pair_out_hbm, atom_out_hbm, token_out_hbm,
-    atom, token, num_in, w_tout, held, token_out,
-    load, done_r, done_w, store,
+    w_tout, token_out,
+    load, done_w, store,
 ):
     col = lax.axis_index("col")
     count = held.shape[0]
-    pairs = [(num_hbm, num_in), (w_tout_hbm, w_tout), (token_hbm, token), (atom_hbm, atom)]
-    loads = [pltpu.make_async_copy(a, b, load.at[i]) for i, (a, b) in enumerate(pairs)]
+    load_w = pltpu.make_async_copy(w_tout_hbm, w_tout, load.at[0])
 
     def rows_of(i):
         return pl.ds(pl.multiple_of((col + 1 + i) % COLS * CHUNK, CHUNK), CHUNK)
-
-    def fetch(i):
-        return pltpu.make_async_copy(done_hbm.at[pl.ds(i * CHUNK, CHUNK)], held.at[i], done_r.at[i])
 
     def hand_on(i):
         return pltpu.make_async_copy(held.at[i], pair_out_hbm.at[rows_of(i)], done_w.at[i])
@@ -463,16 +445,9 @@
         pltpu.make_async_copy(atom, atom_out_hbm, store.at[0]),
         pltpu.make_async_copy(token_out, token_out_hbm, store.at[1]),
     ]
+    load_w.start()
     for i in range(count):
-        fetch(i).start()
-        if i == 1:
-            for copy in loads:
-                copy.start()
-    for i in range(count):
-        fetch(i).wait()
         hand_on(i).start()
-    for copy in loads:
-        copy.wait()
     stores[0].start()
     st = num_in[:, :, 768:].astype(F32)
     tops = st[:, 0:2] + st[:, 2:4] + st[:, 4:6]
@@ -491,6 +466,7 @@
     for s in range(COLS):
         acc = acc + num_in[s, :, :768].astype(F32) * spread[s * OWN:(s + 1) * OWN]
     mix = (acc / spread[COLS * OWN:]).astype(BF16)
+    load_w.wait()
     token_out[...] = (token[...].astype(F32) + dot(mix, w_tout[...])).astype(BF16)
     stores[1].start()
     for i in range(count):
@@ -525,12 +501,9 @@
     atom_out, token_in, num, done = pl.pallas_call(
         step_kernel,
         in_specs=[anywhere] * 14,
-        out_specs=[anywhere] * 4,
+        out_specs=[vmem] * 4,
         out_shape=[
-            jax.ShapeDtypeStruct((128, 128), BF16),
-            jax.ShapeDtypeStruct((OWN, 768), BF16),
-            jax.ShapeDtypeStruct((COLS, OWN, 896), BF16),
-            jax.ShapeDtypeStruct(pair.shape, BF16),
+            pltpu.VMEM((128, 128), BF16), block, mixed, pltpu.VMEM((chunks, *taken), BF16),
         ],
         scratch_shapes=[
             pltpu.VMEM((128, 128), BF16), pltpu.VMEM((128, 128), jnp.int32),
@@ -538,7 +511,6 @@
             pltpu.VMEM((128, 768), BF16), pltpu.VMEM((6, 128), F32),
             pltpu.VMEM((768, 2304), BF16), pltpu.VMEM((1, 256), jnp.int32),
             *pair_args, *prepared,
-            pltpu.VMEM((chunks, *taken), BF16),
             pltpu.VMEM((chunks, *taken), BF16),
             pltpu.VMEM((nq * 16, keys), F32),
             pltpu.VMEM((224, 128), BF16),
@@ -550,8 +522,8 @@
             columns,
             pltpu.VMEM((2, 8, OWN, 768), BF16),
             pltpu.VMEM((128, 768), BF16), keyed, keyed,
-            mixed, mixed, pltpu.VMEM((128, 128), BF16),
-            dma((13,)), dma((3,)), dma((chunks,)), dma((chunks,)),
+            mixed, mixed,
+            dma((13,)), dma((chunks,)),
             dma((2,)), dma((2,)), dma((16,)), dma((16,)), dma((COLS,)), dma((COLS,)),
             dma((COLS,)), dma((COLS,)), dma((16,)), dma((16,)),
             dma((COLS,)), dma((COLS,)),
@@ -566,7 +538,7 @@
     )
     pair_out, atom_out, token_out = pl.pallas_call(
         finish_kernel,
-        in_specs=[anywhere] * 5,
+        in_specs=[vmem] * 4 + [anywhere],
         out_specs=[anywhere] * 3,
         out_shape=[
             jax.ShapeDtypeStruct(pair.shape, BF16),
@@ -574,13 +546,12 @@
             jax.ShapeDtypeStruct((OWN, 768), BF16),
         ],
         scratch_shapes=[
-            pltpu.VMEM((128, 128), BF16), block, mixed, pltpu.VMEM((768, 768), BF16),
-            pltpu.VMEM((chunks, *taken), BF16), block,
-            dma((4,)), dma((chunks,)), dma((chunks,)), dma((2,)),
+            pltpu.VMEM((768, 768), BF16), block,
+            dma((1,)), dma((chunks,)), dma((2,)),
         ],
-        compiler_params=pltpu.CompilerParams(vmem_limit_bytes=VMEM_LIMIT),
+        compiler_params=pltpu.CompilerParams(vmem_limit_bytes=16 << 20),
         name="finish",
-    )(done, atom_out, token_in, num, w_token_out)
+    )(*[pltpu.with_memory_space_constraint(a, pltpu.VMEM) for a in (done, atom_out, token_in, num)], w_token_out)
     return (atom_out, token_out, pair_out)
 
 

time: 59.1 us -> 51.4 us (0.87)
  Pallas kernels: 57.3 us -> 50.2 us
    pallas_call x2, Pallas kernels: 57.3 us -> 50.2 us  [the longest x1 46.5 us: body(): pl.pallas_call(step_kernel, in_specs=[anywhere] * 14, out_specs=[vmem] *...]
where the time goes in v4:
time: 51.4 us; the launch traced here: 51 us
  Pallas kernels  50.2 us (98%)
  between operations  0.82 us (2%)
    pallas_call x1, Pallas kernels, body(): pl.pallas_call(step_kernel, in_specs=[anywhere] * 14, out_specs=[vmem] *...  46.5 us
    pallas_call x1, Pallas kernels, body(): pl.pallas_call(finish_kernel, in_specs=[vmem] * 4 + [anywhere], out_specs...  3.66 us

profile of v4, /device:TPU:0, one launch (start us, length us, event | category | flops | bytes accessed | tf_op | source)
XLA Modules:
  0.0 51.0 jit_solution(3820245052033383404)
XLA Ops:
  0.6 0.0 copy-start
  0.6 46.5 %step.1 = (bf16[128,128]{1,0:T(8,128)(2,1)S(1)}, bf16[16,768]{1,0:T(8,128)(2,1)S(1)}, bf16[8,16,896]{2,1,0:T(8,128)(2,1)S(1)}, bf16[8,16,256,128]{3,2,1,0:T(8,128)(2,1)S(1)}) custom-call(bf16[128,128]{1,0:T(8,128)(2,1)} %atom_hbm.1, s32[128,128]{1,0:T(8,128)} %bitcast.6, bf16[128,384]{1,0:T(8,128)(2,1)} %w_aqkv_hbm.1, bf16[128,128]{1,0:T(8,128)(2,1)} %w_aout_hbm.1, ...), custom_call_target="tpu_custom_call" | custom-call | tf_op jit(solution)/shard_map/step/pallas_call | solution.py:501
  47.2 0.0 copy-done
  47.2 3.7 %finish.1 = (bf16[128,256,128]{2,1,0:T(8,128)(2,1)}, bf16[128,128]{1,0:T(8,128)(2,1)}, bf16[16,768]{1,0:T(8,128)(2,1)}) custom-call(bf16[8,16,256,128]{3,2,1,0:T(8,128)(2,1)S(1)} %get-tuple-element.10.held, bf16[128,128]{1,0:T(8,128)(2,1)S(1)} %get-tuple-element.11.atom, bf16[16,768]{1,0:T(8,128)(2,1)S(1)} %get-tuple-element.12.token, ...), custom_call_target="tpu_custom_call" | custom-call | tf_op jit(solution)/shard_map/finish/pallas_call | solution.py:539
Async XLA Ops:
  0.6 46.5 %copy-start = (bf16[768,768]{1,0:T(8,128)(2,1)S(1)}, bf16[768,768]{1,0:T(8,128)(2,1)}, u32[]{:S(2)}) copy-start(bf16[768,768]{1,0:T(8,128)(2,1)} %w_tout_hbm.1) | copy-start | bytes 3538948

commit v5 on v4

--- a/solution.py
+++ b/solution.py
@@ -18,7 +18,7 @@
 SUM_TYPE = BF16
 CHUNK = 16
 BEFORE = 7
-GROUPS = (4, 3)
+GROUPS = (3, 2, 2)
 STAGES = (0, 1, 3, 5)
 
 

time: 51.4 us -> 51.3 us (level)
  no operation moved by 1% of the time
where the time goes in v5:
time: 51.3 us; the launch traced here: 50.6 us
  Pallas kernels  49.8 us (97%)
  between operations  0.82 us (2%)
    pallas_call x1, Pallas kernels, body(): pl.pallas_call(step_kernel, in_specs=[anywhere] * 14, out_specs=[vmem] *...  46.1 us
    pallas_call x1, Pallas kernels, body(): pl.pallas_call(finish_kernel, in_specs=[vmem] * 4 + [anywhere], out_specs...  3.66 us

profile of v5, /device:TPU:0, one launch (start us, length us, event | category | flops | bytes accessed | tf_op | source)
XLA Modules:
  0.0 50.6 jit_solution(10457832945818334068)
XLA Ops:
  0.6 0.0 copy-start
  0.6 46.1 %step.1 = (bf16[128,128]{1,0:T(8,128)(2,1)S(1)}, bf16[16,768]{1,0:T(8,128)(2,1)S(1)}, bf16[8,16,896]{2,1,0:T(8,128)(2,1)S(1)}, bf16[8,16,256,128]{3,2,1,0:T(8,128)(2,1)S(1)}) custom-call(bf16[128,128]{1,0:T(8,128)(2,1)} %atom_hbm.1, s32[128,128]{1,0:T(8,128)} %bitcast.6, bf16[128,384]{1,0:T(8,128)(2,1)} %w_aqkv_hbm.1, bf16[128,128]{1,0:T(8,128)(2,1)} %w_aout_hbm.1, ...), custom_call_target="tpu_custom_call" | custom-call | tf_op jit(solution)/shard_map/step/pallas_call | solution.py:501
  46.8 0.0 copy-done
  46.8 3.7 %finish.1 = (bf16[128,256,128]{2,1,0:T(8,128)(2,1)}, bf16[128,128]{1,0:T(8,128)(2,1)}, bf16[16,768]{1,0:T(8,128)(2,1)}) custom-call(bf16[8,16,256,128]{3,2,1,0:T(8,128)(2,1)S(1)} %get-tuple-element.10.held, bf16[128,128]{1,0:T(8,128)(2,1)S(1)} %get-tuple-element.11.atom, bf16[16,768]{1,0:T(8,128)(2,1)S(1)} %get-tuple-element.12.token, ...), custom_call_target="tpu_custom_call" | custom-call | tf_op jit(solution)/shard_map/finish/pallas_call | solution.py:539
Async XLA Ops:
  0.6 46.1 %copy-start = (bf16[768,768]{1,0:T(8,128)(2,1)S(1)}, bf16[768,768]{1,0:T(8,128)(2,1)}, u32[]{:S(2)}) copy-start(bf16[768,768]{1,0:T(8,128)(2,1)} %w_tout_hbm.1) | copy-start | bytes 3538948
